TPU v7x, 128 devices: a whole 4x4x4 slice. The times are simulated.
128 devices in a mesh: dp: 2 (over y_lo), ctx: 16 (over x, z), exp: 4 (over y_hi, core).
Axes of the slice: x: 4, y: 4 (y_hi: 2, y_lo: 2; y = y_hi * 2 + y_lo), z: 4, core: 2. Of those that a mesh axis runs over, the one named last changes fastest.
Arguments:
- tokens: bfloat16 [8, 2048, 1024], P(('dp', 'exp'), 'ctx'), may hold values from -6 to 6
- places: int32 [8, 2048], P(('dp', 'exp')), may hold values from 0 to 2047, as said below
- choices: int32 [8, 2048, 8], P(('dp', 'exp'), 'ctx'), may hold values from 0 to 31, all different within a row; in each aligned block of 128 rows (0 to 127, 128 to 255, ..., all dimensions but the last counted through in order) at most 40 rows name the same one
- cotangent: bfloat16 [8, 2048, 1024], P(('dp', 'exp'), 'ctx'), may hold values from -6 to 6
- attn_gain: bfloat16 [1024], replicated, may hold values from 0.25 to 1.75
- w_query: bfloat16 [1024, 1024], replicated, may hold values from -0.1875 to 0.1875
- w_key: bfloat16 [1024, 512], replicated, may hold values from -0.1875 to 0.1875
- w_value: bfloat16 [1024, 512], replicated, may hold values from -0.1875 to 0.1875
- query_gain: bfloat16 [1024], replicated, may hold values from 0.25 to 1.75
- key_gain: bfloat16 [512], replicated, may hold values from 0.25 to 1.75
- w_out: bfloat16 [1024, 1024], replicated, may hold values from -1.5 to 1.5
- ffn_gain: bfloat16 [1024], replicated, may hold values from 0.25 to 1.75
- w_router: bfloat16 [1024, 32], replicated, may hold values from -0.09375 to 0.09375
- w_gate: bfloat16 [32, 1024, 512], P('ctx', None, 'exp'), may hold values from -0.1875 to 0.1875
- w_up: bfloat16 [32, 1024, 512], P('ctx', None, 'exp'), may hold values from -0.1875 to 0.1875
- w_down: bfloat16 [32, 512, 1024], P('ctx', 'exp'), may hold values from -2 to 2
Outputs:
- out: bfloat16 [8, 2048, 1024], P(('dp', 'exp'), 'ctx')
- input_grad: float32 [8, 2048, 1024], P(('dp', 'exp'), 'ctx')
- attn_gain_grad: float32 [1024], replicated
- w_query_grad: float32 [1024, 1024], replicated
- w_key_grad: float32 [1024, 512], replicated
- w_value_grad: float32 [1024, 512], replicated
- query_gain_grad: float32 [1024], replicated
- key_gain_grad: float32 [512], replicated
- w_out_grad: float32 [1024, 1024], replicated
- ffn_gain_grad: float32 [1024], replicated
- w_router_grad: float32 [1024, 32], replicated
- w_gate_grad: float32 [32, 1024, 512], P('ctx', None, 'exp')
- w_up_grad: float32 [32, 1024, 512], P('ctx', None, 'exp')
- w_down_grad: float32 [32, 512, 1024], P('ctx', 'exp')
Inputs may be any that keep to these rules, and one draw needn't show every extreme that they name: Each row of places is a permutation of the positions of its sequence. Split a sequence into 32 runs of 64 consecutive positions; token slots 128 * c to 128 * (c + 1) - 1 hold, in slot order, run b and run 2 * 16 - 1 - b (in either order) for some b, each run ascending. `choices`: each token names 8 different experts. Among the tokens of one device (aligned blocks of 128 token slots of a sequence) no expert is named more than 40 times, a bound that some block reaches.
All inputs are finite; a program needn't handle non-finite values.
Results may differ from a plain program's by a relative error of at most 0.024.
Values may be sent and summed in bfloat16 or wider, within the bound.
No kernel may reach another device: no remote copies, remote signals or barrier semaphores. Data moves between devices by JAX's collectives and lax.ppermute only.
A program may use at most 256 MiB of HBM per device.

v0:
```python
import jax
import jax.numpy as jnp
import numpy as np
from jax import lax
from jax.experimental import pallas as pl
from jax.experimental.pallas import tpu as pltpu
from jax.sharding import PartitionSpec as P

HEADS = 16
KV_HEADS = 8
HEAD_DIM = 64
EXPERTS = 32
CAP = 40
EPSILON = 1e-06
MASKED = -1e30
BF = jnp.bfloat16
F32 = jnp.float32
RUN = 64
QB = 512
QB_BACK = 256
PART = 208
BASE = 256
MIB = 1024 * 1024
NT = ((1,), (1,))
TN = ((0,), (0,))
VM = pl.BlockSpec(memory_space=pltpu.VMEM)
SM = pl.BlockSpec(memory_space=pltpu.SMEM)


def dot(a, b, dims=((1,), (0,))):
    return lax.dot_general(a, b, (dims, ((), ())), preferred_element_type=F32)


def call(kernel, outs, ins, name, flops, moved, scratch=(), transcendentals=0, vmem=62):
    return pl.pallas_call(
        kernel,
        out_shape=outs,
        in_specs=ins,
        out_specs=jax.tree.map(lambda _: VM, outs),
        scratch_shapes=list(scratch),
        compiler_params=pltpu.CompilerParams(vmem_limit_bytes=vmem * MIB),
        cost_estimate=pl.CostEstimate(
            flops=flops, bytes_accessed=moved, transcendentals=transcendentals
        ),
        name=name,
    )


def like(shape, dtype):
    return jax.ShapeDtypeStruct(shape, dtype)


def inverse_rms(value):
    return lax.rsqrt(jnp.mean(value * value, axis=-1, keepdims=True) + EPSILON)


def row_of(ref):
    return ref[...].astype(F32).reshape(1, -1)


def lanes_of(rows):
    return lax.broadcasted_iota(jnp.int32, (rows, 128), 1)


def swap_halves(tile):
    return pltpu.roll(tile.astype(F32), 64, 1)


def pack_head(wide, head):
    tile = wide[:, 128 * (head // 2) : 128 * (head // 2 + 1)]
    low = lanes_of(RUN) < 64
    if head % 2 == 0:
        return jnp.where(low, tile[:RUN], swap_halves(tile[RUN:]))
    return jnp.where(low, swap_halves(tile[:RUN]), tile[RUN:])


def unpack_heads(even, odd):
    low = lanes_of(RUN) < 64
    even, odd = even.astype(F32), odd.astype(F32)
    return jnp.concatenate(
        [jnp.where(low, even, swap_halves(odd)), jnp.where(low, swap_halves(even), odd)], axis=0
    )


def turn_tables(seq):
    half = HEAD_DIM // 2
    frequency = (10000.0 ** (-np.arange(half) * 2.0 / HEAD_DIM)).astype(np.float32)
    angles = (np.arange(seq, dtype=np.float32)[:, None] * frequency[None, :]).astype(np.float64)
    cosine, sine = np.cos(angles), np.sin(angles)
    return np.concatenate([cosine, cosine, -sine, sine], axis=1).astype(np.float32)


def split_table(table):
    low = lanes_of(table.shape[0]) < 64
    return jnp.where(low, table, 1.0), jnp.where(low, pltpu.roll(table, 64, 1), 0.0)


def turn(tile, cosine, sine):
    other = jnp.where(lanes_of(tile.shape[0]) < 32, pltpu.roll(tile, 96, 1), pltpu.roll(tile, 32, 1))
    return tile * cosine + other * sine


def pre_kernel(x_ref, gain, wq, wk, wv, q_gain, k_gain, picks, send, first_out, turned_out, q_out, k_out):
    x = x_ref[...].astype(F32)
    wide = x * inverse_rms(x) * row_of(gain)
    first = wide.astype(BF)
    first_out[...] = first
    q = dot(first, wq[...])
    k = dot(first, wk[...])
    v = dot(first, wv[...])
    q_out[...] = q
    k_out[...] = k
    qn = q * inverse_rms(q) * (row_of(q_gain) * HEAD_DIM ** (-0.5))
    kn = k * inverse_rms(k) * row_of(k_gain)
    low = lanes_of(x.shape[0]) < 64
    for h in range(KV_HEADS):
        cut = slice(128 * (h // 2), 128 * (h // 2 + 1))
        kt, vt = kn[:, cut], v[:, cut]
        if h % 2 == 0:
            both = jnp.where(low, kt, swap_halves(vt))
        else:
            both = jnp.where(low, swap_halves(kt), vt)
        both = both.astype(BF)
        send[2 * h, 0 : 2 * RUN, :] = both
        send[2 * h + 1, 0 : 2 * RUN, :] = both
    lane = lanes_of(x.shape[0])
    rows = jnp.transpose(jnp.where(lane == 0, inverse_rms(q), inverse_rms(k)))[0:2, :]
    high = rows.astype(BF).astype(F32)
    named = jnp.concatenate(
        [picks[...].astype(F32), high, rows - high, jnp.zeros((4, 128), F32)], axis=0
    ).astype(BF)
    for d in range(HEADS):
        send[d, 2 * RUN : 3 * RUN, :] = pack_head(qn, d).astype(BF)
        send[d, 3 * RUN : 3 * RUN + 16, :] = named
    turned_out[...] = jnp.transpose(first.astype(F32)).astype(BF)


def pre(x, gain, wq, wk, wv, q_gain, k_gain, picks):
    rows, width = x.shape
    return call(
        pre_kernel,
        (
            like((HEADS, 3 * RUN + 16, 128), BF),
            like((rows, width), BF),
            like((width, rows), BF),
            like((rows, wq.shape[1]), F32),
            like((rows, wk.shape[1]), F32),
        ),
        [VM] * 8,
        "pre",
        2 * rows * width * 2048,
        6 * 1024 * 1024,
    )(x, gain, wq, wk, wv, q_gain, k_gain, picks)


def turn_over(source, target):
    for i in range(source.shape[0] // 128):
        cut = slice(128 * i, 128 * (i + 1))
        target[:, cut] = jnp.transpose(source[cut, :].astype(F32)).astype(BF)


def masked_scores(kv, q, block):
    scores = dot(kv, q, NT)
    end = scores.shape[0]
    row = lax.broadcasted_iota(jnp.int32, (block, block), 0)
    col = lax.broadcasted_iota(jnp.int32, (block, block), 1)
    last = jnp.where(row <= col, scores[end - block :, :], MASKED)
    return last if end == block else jnp.concatenate([scores[: end - block, :], last], axis=0)


def attend_kernel(order, inv, recv, table, kv_out, q_out, att_out, lse_out, send_out, turned):
    seq = kv_out.shape[0]
    lane = lanes_of(RUN)

    def gather(b, carry):
        s = order[b]
        c = lax.shift_right_logical(s, 1)
        half = jnp.bitwise_and(s, 1)
        rows = pl.ds(pl.multiple_of(b * RUN, RUN), RUN)
        cos, sin = split_table(table[rows, :])
        kv = recv[c, pl.ds(pl.multiple_of(half * RUN, RUN), RUN), :].astype(F32)
        kv_out[rows, :] = turn(kv, cos, sin).astype(BF)
        tile = recv[c, pl.ds(2 * RUN, RUN), :].astype(F32)
        q = jnp.where(lane < 64, jnp.where(half == 0, tile, swap_halves(tile)), 0.0)
        q_out[rows, :] = turn(q, cos, sin).astype(BF)
        return carry

    lax.fori_loop(0, seq // RUN, gather, 0, unroll=32)
    turn_over(kv_out, turned)
    for i in range(seq // QB):
        here = slice(i * QB, (i + 1) * QB)
        end = (i + 1) * QB
        scores = masked_scores(kv_out[:end, :], q_out[here, :], QB)
        top = jnp.max(scores, axis=0, keepdims=True)
        weights = jnp.exp(scores - top)
        total = jnp.sum(weights, axis=0, keepdims=True)
        att = jnp.transpose(dot(turned[:, :end], weights.astype(BF)) / total)
        att_out[here, :] = att.astype(BF)
        lse_out[:, here] = jnp.broadcast_to(top + jnp.log(total), (8, QB))

    def place(c, carry):
        b0, b1 = inv[2 * c], inv[2 * c + 1]
        first = att_out[pl.ds(pl.multiple_of(b0 * RUN, RUN), RUN), :]
        second = att_out[pl.ds(pl.multiple_of(b1 * RUN, RUN), RUN), :]
        send_out[c] = jnp.where(lane < 64, swap_halves(first), second.astype(F32)).astype(BF)
        return carry

    lax.fori_loop(0, send_out.shape[0], place, 0, unroll=16)


def attend(order, inv, recv, table):
    n = recv.shape[0]
    seq = n * 128
    return call(
        attend_kernel,
        (
            like((seq, 128), BF),
            like((seq, 128), BF),
            like((seq, 128), BF),
            like((8, seq), F32),
            like((n, RUN, 128), BF),
        ),
        [SM, SM, VM, VM],
        "attend",
        4 * seq * seq * 128 // 2,
        14 * seq * 128,
        [pltpu.VMEM((128, seq), BF)],
        transcendentals=seq * seq // 2,
    )(order, inv, recv, table)


def attend_back_kernel(
    order, inv, even, recv, kv_in, q_in, att_in, lse_in, table, _,
    send_hbm, kv_grad_out, g_all, dq_all, dkv_all, sums, turned, send_out, sem,
):
    seq = kv_in.shape[0]
    lane = lanes_of(RUN)

    def gather(b, carry):
        s = order[b]
        c = lax.shift_right_logical(s, 1)
        half = jnp.bitwise_and(s, 1)
        tile = recv[c, 0:RUN, :].astype(F32)
        g_all[pl.ds(pl.multiple_of(b * RUN, RUN), RUN), :] = jnp.where(
            lane >= 64, jnp.where(half == 1, tile, swap_halves(tile)), 0.0
        ).astype(BF)
        return carry

    lax.fori_loop(0, seq // RUN, gather, 0, unroll=32)
    turn_over(kv_in, turned)
    steps = seq // QB_BACK
    for i in reversed(range(steps)):
        here = slice(i * QB_BACK, (i + 1) * QB_BACK)
        end = (i + 1) * QB_BACK
        kv, q, g = kv_in[:end, :], q_in[here, :], g_all[here, :]
        offset = jnp.sum(jnp.transpose(att_in[here, :].astype(F32) * g.astype(F32)), axis=0, keepdims=True)
        weights = jnp.exp(masked_scores(kv, q, QB_BACK) - lse_in[0:1, here])
        grad_scores = (weights * (dot(kv, g, NT) - offset)).astype(BF)
        dq_all[here, :] = jnp.transpose(dot(turned[:, :end], grad_scores))
        step = dot(grad_scores, q) + dot(weights.astype(BF), g)
        if i == steps - 1:
            dkv_all[...] = step
        else:
            dkv_all[:end, :] += step

    def place(c, carry):
        b0, b1 = inv[2 * c], inv[2 * c + 1]
        r0 = pl.ds(pl.multiple_of(b0 * RUN, RUN), RUN)
        r1 = pl.ds(pl.multiple_of(b1 * RUN, RUN), RUN)
        cos0, sin0 = split_table(table[r0, :])
        cos1, sin1 = split_table(table[r1, :])
        kv0 = turn(dkv_all[r0, :], cos0, -sin0).astype(BF)
        kv1 = turn(dkv_all[r1, :], cos1, -sin1).astype(BF)
        send_out[c, 0 : RUN, :] = kv0
        send_out[c, RUN : 2 * RUN, :] = kv1
        kv0, kv1 = kv0.astype(F32), kv1.astype(F32)
        values = jnp.where(lane < 64, swap_halves(kv0), kv1)
        keys = jnp.where(lane < 64, kv0, swap_halves(kv1))
        kv_grad_out[c] = jnp.where(even[0] == 1, values, keys).astype(BF)
        both_q = jnp.concatenate([dq_all[r0, :], dq_all[r1, :]], axis=0)
        both_q = both_q * jnp.concatenate([q_in[r0, :], q_in[r1, :]], axis=0).astype(F32)
        both_k = jnp.concatenate([dkv_all[r0, :], dkv_all[r1, :]], axis=0)
        both_k = both_k * jnp.concatenate([kv_in[r0, :], kv_in[r1, :]], axis=0).astype(F32)
        some = jnp.where(lanes_of(8) < 64, 1.0, 0.0).astype(BF)
        sums[pl.ds(c, 1), :] = dot(some, both_q.astype(BF), NT)[0:1, :]
        sums[pl.ds(n + c, 1), :] = dot(some, both_k.astype(BF), NT)[0:1, :]
        q0 = turn(dq_all[r0, :], cos0, -sin0)
        q1 = turn(dq_all[r1, :], cos1, -sin1)
        both = jnp.where(lane < 64, q0, swap_halves(q1))
        send_out[c, 2 * RUN : 3 * RUN, :] = (both * HEAD_DIM ** (-0.5)).astype(BF)
        return carry

    n = send_out.shape[0]
    lax.fori_loop(0, n, place, 0, unroll=16)
    for c in range(n):
        send_out[c, 3 * RUN : 3 * RUN + 2 * n, :] = sums[...].astype(BF)
    copy = pltpu.make_async_copy(send_out, send_hbm.at[:, pl.ds(BASE, 3 * RUN + 2 * n), :], sem)
    copy.start()
    copy.wait()


def attend_back(order, inv, even, recv, kv, q, att, lse, table, begun):
    n = recv.shape[0]
    seq = n * 128
    whole = lambda v: pl.BlockSpec(v.shape, lambda i: (0,) * v.ndim)
    return pl.pallas_call(
        attend_back_kernel,
        grid=(1,),
        out_shape=(like((n, BASE + 3 * RUN + 2 * n, 128), BF), like((n, RUN, 128), BF)),
        in_specs=[SM, SM, SM]
        + [whole(v) for v in (recv, kv, q, att, lse, table)]
        + [pl.BlockSpec(memory_space=pl.ANY)],
        input_output_aliases={9: 0},
        out_specs=(
            pl.BlockSpec(memory_space=pl.ANY),
            pl.BlockSpec((n, RUN, 128), lambda i: (0, 0, 0)),
        ),
        scratch_shapes=[
            pltpu.VMEM((seq, 128), BF),
            pltpu.VMEM((seq, 128), F32),
            pltpu.VMEM((seq, 128), F32),
            pltpu.VMEM((2 * n, 128), F32),
            pltpu.VMEM((128, seq), BF),
            pltpu.VMEM((n, 3 * RUN + 2 * n, 128), BF),
            pltpu.SemaphoreType.DMA,
        ],
        compiler_params=pltpu.CompilerParams(vmem_limit_bytes=62 * MIB),
        cost_estimate=pl.CostEstimate(
            flops=10 * seq * seq * 128 // 2, bytes_accessed=20 * seq * 128, transcendentals=seq * seq // 2
        ),
        name="attend_back",
    )(order, inv, even, recv, kv, q, att, lse, table, begun)


def slot_masks(slot, pair):
    line = lax.broadcasted_iota(jnp.int32, (2 * CAP, 128), 0).astype(F32)
    left = (line < CAP) & (line == slot[2 * pair : 2 * pair + 1, :])
    right = (line >= CAP) & (line - CAP == slot[2 * pair + 1 : 2 * pair + 2, :])
    return jnp.where(left, 1.0, 0.0).astype(BF), jnp.where(right, 1.0, 0.0).astype(BF)


def cotangent_kernel(number, picks_ref, g_ref, rows_ref, slot_ref):
    n_ctx = g_ref.shape[0]
    picks = picks_ref[...].astype(F32)[:, :8, :]
    before = lax.broadcasted_iota(jnp.int32, (128, 128), 0) < lax.broadcasted_iota(
        jnp.int32, (128, 128), 1
    )
    before = jnp.where(before, 1.0, 0.0).astype(BF)
    for a in range(2):
        e = (number[0] + a).astype(F32)
        named = jnp.max(jnp.where(picks == e, 1.0, 0.0), axis=1)
        slot = jnp.where(named > 0.0, dot(named.astype(BF), before), -1.0)
        slot_ref[a] = slot
        for p in range(n_ctx // 2):
            left, right = slot_masks(slot, p)
            rows_ref[a, 2 * CAP * p : 2 * CAP * (p + 1), :] = (
                dot(left, g_ref[2 * p]) + dot(right, g_ref[2 * p + 1])
            ).astype(BF)


def cotangent_rows(number, recv, g_all):
    n_ctx = g_all.shape[0]
    whole = lambda *shape: pl.BlockSpec(shape, lambda i: (0,) * len(shape))
    return pl.pallas_call(
        cotangent_kernel,
        grid=(1,),
        out_shape=(like((2, n_ctx * CAP, 1024), BF), like((2, n_ctx, 128), F32)),
        in_specs=[
            SM,
            pl.BlockSpec((n_ctx, 16, 128), lambda i: (0, 3 * RUN // 16, 0)),
            whole(*g_all.shape),
        ],
        out_specs=(whole(2, n_ctx * CAP, 1024), whole(2, n_ctx, 128)),
        compiler_params=pltpu.CompilerParams(vmem_limit_bytes=62 * MIB),
        cost_estimate=pl.CostEstimate(
            flops=8 * n_ctx * 80 * 128 * 1024, bytes_accessed=8 * 1024 * 1024, transcendentals=0
        ),
        name="cotangent_rows",
    )(number, recv, g_all)


def expert_steps(e, rows_ref, g_ref, router_ref, parts):
    n_ctx = rows_ref.shape[0]
    rows = jnp.concatenate([rows_ref[c, 0].astype(F32) for c in range(n_ctx)], axis=0).astype(BF)
    grads = g_ref[0].astype(F32)
    logits = dot(rows, router_ref[...], NT)
    lane = lax.broadcasted_iota(jnp.int32, logits.shape, 1)
    powers = jnp.exp(logits - jnp.max(logits, axis=1, keepdims=True))
    gate = jnp.sum(jnp.where(lane == e, powers, 0.0), axis=1, keepdims=True) / jnp.sum(
        powers, axis=1, keepdims=True
    )
    w_gate = jnp.concatenate([w[0, 0:1024, :] for w in parts], axis=1)
    w_up = jnp.concatenate([w[0, 1024:2048, :] for w in parts], axis=1)
    w_down = jnp.concatenate(
        [
            jnp.concatenate([w[0, 2048 + 128 * n : 2176 + 128 * n, :] for n in range(8)], axis=1)
            for w in parts
        ],
        axis=0,
    )
    gate_act = dot(rows, w_gate)
    up_act = dot(rows, w_up)
    sig = 1.0 / (1.0 + jnp.exp(-gate_act))
    silu = gate_act * sig
    hidden = (silu * up_act).astype(BF)
    expert_out = dot(hidden, w_down)
    grad_rows = (gate * grads).astype(BF)
    grad_hidden = dot(grad_rows, w_down, NT)
    ga = (grad_hidden * up_act * sig * (1.0 + gate_act * (1.0 - sig))).astype(BF)
    gu = (grad_hidden * silu).astype(BF)
    return rows, grads, gate, w_gate, w_up, hidden, expert_out, grad_rows, ga, gu


def expert_kernel(number, rows_ref, g_ref, router_ref, *refs):
    parts, back_ref = refs[:4], refs[4]
    e = number[0] + pl.program_id(0)
    rows, grads, _, w_gate, w_up, _, expert_out, _, ga, gu = expert_steps(
        e, rows_ref, g_ref, router_ref, parts
    )
    grad_gate = jnp.sum(grads * expert_out, axis=1, keepdims=True)
    back = dot(ga, w_gate, NT) + dot(gu, w_up, NT)
    high = grad_gate.astype(BF).astype(F32)
    lane = lanes_of(rows.shape[0])
    tail = jnp.where(lane == e, high, jnp.where(lane == e + EXPERTS, grad_gate - high, 0.0))
    for c in range(rows_ref.shape[0]):
        cut = slice(CAP * c, CAP * (c + 1))
        back_ref[c, 0, :, 0:1024] = back[cut, :].astype(BF)
        back_ref[c, 0, :, 1024:1152] = tail[cut, :].astype(BF)


def weight_grad_kernel(number, rows_ref, g_ref, router_ref, slot_ref, *refs):
    parts, (keep, near, far, sums_ref) = refs[:4], refs[4:]
    e = number[0] + pl.program_id(0)
    rows, _, gate, _, _, hidden, expert_out, grad_rows, ga, gu = expert_steps(
        e, rows_ref, g_ref, router_ref, parts
    )
    line = lax.broadcasted_iota(jnp.int32, (CAP, 128), 0).astype(F32)
    first = pl.program_id(0) == 0
    out_rows = gate * expert_out
    for c in range(rows_ref.shape[0]):
        mask = jnp.where(line == slot_ref[0, c : c + 1, :], 1.0, 0.0).astype(BF)
        part = dot(mask, out_rows[CAP * c : CAP * (c + 1), :].astype(BF), TN)
        before = jnp.where(first, 0.0, sums_ref[c].astype(F32))
        sums_ref[c] = (part + before).astype(BF)
    gate_grad = dot(rows, ga, TN)
    up_grad = dot(rows, gu, TN)
    down_grad = dot(hidden, grad_rows, TN)
    for j, (ref, at) in enumerate([(keep, 0), (far, 0), (near, 0), (far, 1)]):
        cut = slice(128 * j, 128 * (j + 1))
        ref[at, 0, 0:1024, :] = gate_grad[:, cut].astype(BF)
        ref[at, 0, 1024:2048, :] = up_grad[:, cut].astype(BF)
        for n in range(8):
            ref[at, 0, 2048 + 128 * n : 2176 + 128 * n, :] = down_grad[
                cut, 128 * n : 128 * (n + 1)
            ].astype(BF)


def expert_call(kernel, name, number, rows, grads, router, slots, parts, outs, out_specs):
    n_ctx = rows.shape[0]
    n = n_ctx * CAP
    extra = () if slots is None else (slots,)
    return pl.pallas_call(
        kernel,
        grid=(2,),
        out_shape=outs,
        in_specs=[
            SM,
            pl.BlockSpec((n_ctx, 1, CAP, 1024), lambda i: (0, i, 0, 0)),
            pl.BlockSpec((1, n, 1024), lambda i: (i, 0, 0)),
            pl.BlockSpec(router.shape, lambda i: (0, 0)),
        ]
        + [pl.BlockSpec((1,) + v.shape[1:], lambda i: (i, 0, 0)) for v in extra + tuple(parts)],
        out_specs=out_specs,
        compiler_params=pltpu.CompilerParams(vmem_limit_bytes=62 * MIB),
        cost_estimate=pl.CostEstimate(
            flops=24 * n * 1024 * 512, bytes_accessed=20 * 1024 * 1024, transcendentals=2 * n * 512
        ),
        name=name,
    )(number, rows, grads, router, *extra, *parts)


def experts(number, rows, grads, router, parts):
    n_ctx = rows.shape[0]
    return expert_call(
        expert_kernel, "experts", number, rows, grads, router, None, parts,
        like((n_ctx, 2, CAP, 1152), BF),
        pl.BlockSpec((n_ctx, 1, CAP, 1152), lambda i: (0, i, 0, 0)),
    )


def weight_grads(number, rows, grads, router, slots, parts):
    n_ctx = rows.shape[0]
    put = lambda k: pl.BlockSpec((k, 1, 3072, 128), lambda i: (0, i, 0, 0))
    return expert_call(
        weight_grad_kernel, "weight_grads", number, rows, grads, router, slots, parts,
        (
            like((1, 2, 3072, 128), BF),
            like((1, 2, 3072, 128), BF),
            like((2, 2, 3072, 128), BF),
            like((n_ctx, 128, 1024), BF),
        ),
        (put(1), put(1), put(2), pl.BlockSpec((n_ctx, 128, 1024), lambda i: (0, 0, 0))),
    )


def middle_kernel(heads, x_ref, w_out, gain, spot, attended_out, middle_out, second_out, send_out):
    attended = jnp.concatenate(
        [unpack_heads(heads[2 * t], heads[2 * t + 1]) for t in range(HEADS // 2)], axis=1
    ).astype(BF)
    attended_out[...] = attended
    middle = x_ref[...].astype(F32) + dot(attended, w_out[...])
    middle_out[...] = middle
    second = (middle * inverse_rms(middle) * row_of(gain)).astype(BF)
    second_out[...] = second
    send_out[...] = dot(spot[...], second, TN).astype(BF)


def middle_forward(heads, x, w_out, gain, spot):
    rows, width = x.shape
    return call(
        middle_kernel,
        (
            like((rows, width), BF),
            like((rows, width), F32),
            like((rows, width), BF),
            like((spot.shape[1], width), BF),
        ),
        [VM] * 5,
        "middle",
        2 * rows * width * (1024 + 1280),
        6 * 1024 * 1024,
    )(heads, x, w_out, gain, spot)


def middle_back_kernel(
    spot, back, middle_ref, second, router, gain, g_ref, w_out,
    send, grad_out, branch_out,
):
    summed = dot(spot[...], back[...])
    logits = dot(second[...], router[...], NT)
    powers = jnp.exp(logits - jnp.max(logits, axis=1, keepdims=True))
    probs = powers / jnp.sum(powers, axis=1, keepdims=True)
    last = summed[:, 1024:1152]
    grad_sel = (last + pltpu.roll(last, 128 - EXPERTS, 1))[:, :EXPERTS]
    grad_logits = probs * (grad_sel - jnp.sum(probs * grad_sel, axis=1, keepdims=True))
    high = grad_logits.astype(BF)
    rest = (grad_logits - high.astype(F32)).astype(BF)
    upstream = summed[:, :1024] + dot(high, router[...]) + dot(rest, router[...])
    middle = middle_ref[...]
    r = inverse_rms(middle)
    hat = middle * r
    gain_part = jnp.sum(upstream * hat, axis=0, keepdims=True)
    router_part = dot(high, second[...], TN) + dot(rest, second[...], TN)
    low = lanes_of(EXPERTS) < 64
    first_row = lax.broadcasted_iota(jnp.int32, (EXPERTS, 128), 0) == 0
    for d in range(HEADS):
        cut = slice(128 * (d // 2), 128 * (d // 2 + 1))
        tile = router_part[:, cut]
        part = jnp.where(first_row, jnp.broadcast_to(gain_part[:, cut], (EXPERTS, 128)), 0.0)
        if d % 2 == 0:
            misc = jnp.where(low, tile, swap_halves(part))
        else:
            misc = jnp.where(low, swap_halves(tile), part)
        send[d, RUN : RUN + EXPERTS, :] = misc.astype(BF)
    scaled = upstream * row_of(gain)
    grad = (
        r * (scaled - hat * jnp.mean(scaled * hat, axis=1, keepdims=True)) + g_ref[...].astype(F32)
    )
    grad_out[...] = grad
    branch = grad.astype(BF)
    branch_out[...] = branch
    att = dot(branch, w_out[...], NT)
    for d in range(HEADS):
        send[d, 0:RUN, :] = pack_head(att, d).astype(BF)


def middle_back(spot, back, middle, second, router, gain, g_low, w_out):
    rows, width = middle.shape
    return call(
        middle_back_kernel,
        (
            like((HEADS, RUN + EXPERTS, 128), BF),
            like((rows, width), F32),
            like((rows, width), BF),
        ),
        [VM] * 8,
        "middle_back",
        2 * rows * width * (1280 + 1024),
        6 * 1024 * 1024,
    )(spot, back, middle, second, router, gain, g_low, w_out)


def out_grad_kernel(place, attended, other, branch, other_branch, send_hbm, rows, sem):
    for j in range(4):
        pair = jnp.bitwise_xor(place[0], j % 2) * 2 + jnp.bitwise_xor(place[1], j // 2)
        own = attended[:, pl.ds(pl.multiple_of((2 * pair + place[2]) * 128, 128), 128)]
        far = other[:, pl.ds(pl.multiple_of(pair * 128, 128), 128)]
        part = dot(own, branch[...], TN) + dot(far, other_branch[...], TN)
        for c in range(rows.shape[0]):
            both = part[8 * c : 8 * c + 8, :]
            for m in range(0, 8, 2):
                two = (both[:, 128 * m : 128 * m + 128], both[:, 128 * m + 128 : 128 * m + 256])
                at = 64 * j + 8 * m
                rows[c, at : at + 16, :] = jnp.concatenate(two, axis=0).astype(BF)
    copy = pltpu.make_async_copy(rows, send_hbm.at[:, pl.ds(0, BASE), :], sem)
    copy.start()
    copy.wait()


def out_grads(place, attended, other, branch, other_branch):
    n = HEADS
    whole = lambda v: pl.BlockSpec(v.shape, lambda i: (0,) * v.ndim)
    return pl.pallas_call(
        out_grad_kernel,
        grid=(1,),
        out_shape=like((n, BASE + 3 * RUN + 2 * n, 128), BF),
        in_specs=[SM] + [whole(v) for v in (attended, other, branch, other_branch)],
        out_specs=pl.BlockSpec(memory_space=pl.ANY),
        scratch_shapes=[pltpu.VMEM((n, BASE, 128), BF), pltpu.SemaphoreType.DMA],
        compiler_params=pltpu.CompilerParams(vmem_limit_bytes=62 * MIB),
        cost_estimate=pl.CostEstimate(flops=1 << 20, bytes_accessed=1 << 18, transcendentals=0),
        name="out_grads",
    )(place, attended, other, branch, other_branch)


def queries_of(recv):
    return jnp.concatenate(
        [
            unpack_heads(
                recv[2 * t, BASE + 2 * RUN : BASE + 3 * RUN, :],
                recv[2 * t + 1, BASE + 2 * RUN : BASE + 3 * RUN, :],
            )
            for t in range(HEADS // 2)
        ],
        axis=1,
    )


def keys_values_of(recv):
    low = lanes_of(2 * RUN) < 64
    both = [
        recv[2 * j, BASE : BASE + 2 * RUN, :].astype(F32)
        + recv[2 * j + 1, BASE : BASE + 2 * RUN, :].astype(F32)
        for j in range(KV_HEADS)
    ]
    keys, values = [], []
    for t in range(KV_HEADS // 2):
        keys.append(jnp.where(low, both[2 * t], swap_halves(both[2 * t + 1])))
        values.append(jnp.where(low, swap_halves(both[2 * t]), both[2 * t + 1]))
    return jnp.concatenate(keys, axis=1), jnp.concatenate(values, axis=1)


def input_kernel(
    recv, q_ref, k_ref, x_ref, middle, q_gain, k_gain, gain, wq, wk, wv, out_ref, gain_ref
):
    uq = queries_of(recv)
    uk, dv = keys_values_of(recv)
    q, k = q_ref[...], k_ref[...]
    rq, rk = inverse_rms(q), inverse_rms(k)
    qh, kh = q * rq, k * rk
    uq, uk = uq * row_of(q_gain), uk * row_of(k_gain)
    gq = (rq * (uq - qh * jnp.mean(uq * qh, axis=1, keepdims=True))).astype(BF)
    gk = (rk * (uk - kh * jnp.mean(uk * kh, axis=1, keepdims=True))).astype(BF)
    upstream = dot(gq, wq[...], NT) + dot(gk, wk[...], NT) + dot(dv.astype(BF), wv[...], NT)
    x = x_ref[...].astype(F32)
    r = inverse_rms(x)
    hat = x * r
    x_part = jnp.sum(upstream * hat, axis=0, keepdims=True)
    scaled = upstream * row_of(gain)
    out_ref[...] = middle[...] + r * (scaled - hat * jnp.mean(scaled * hat, axis=1, keepdims=True))
    half = jnp.zeros((1, 64), F32)
    rows = [jnp.concatenate([half, x_part[:, 64 * i : 64 * (i + 1)]], axis=1) for i in range(8)]
    none = jnp.zeros((2, 128), F32)
    more = [x_part[:, 512 + 128 * i : 640 + 128 * i] for i in range(4)]
    gain_ref[...] = jnp.concatenate(rows + [none] + more + [none], axis=0)


def input_back(recv, q, k, x, middle, q_gain, k_gain, gain, wq, wk, wv):
    rows, width = x.shape
    return call(
        input_kernel,
        (like((rows, width), F32), like((16, 128), F32)),
        [VM] * 11,
        "input_back",
        2 * rows * width * 2048,
        8 * 1024 * 1024,
    )(recv, q, k, x, middle, q_gain, k_gain, gain, wq, wk, wv)


def head_grad_kernel(
    place, turned, early, later, queries, kv_other, normed, out_parts, sums_ref, branch, gain_ref, out_ref
):
    n = early.shape[0]
    low = lanes_of(128) < 64
    gain = gain_ref[...]
    sums = sums_ref[0].astype(F32)
    others = branch[0].astype(F32)
    for c in range(1, n):
        sums = sums + sums_ref[c].astype(F32)
        others = others + branch[c].astype(F32)
    out_rows = out_parts[0].astype(F32)
    for c in range(1, n):
        out_rows = out_rows + out_parts[c].astype(F32)
    q_means = sums[0:n, :] / (HEADS * HEAD_DIM)
    k_means = sums[n : 2 * n, :] / (KV_HEADS * HEAD_DIM)
    total = None
    gains = None
    for p in range(n // 2):
        parts = []
        for c in (2 * p, 2 * p + 1):
            packed = queries[c].astype(F32)
            uq = jnp.concatenate([packed, swap_halves(packed)], axis=0)
            both = jnp.concatenate([early[c].astype(F32), later[c].astype(F32)], axis=0)
            other = kv_other[c].astype(F32)
            other = jnp.concatenate([swap_halves(other), other], axis=0)
            keys = swap_halves(both) + other
            upstream = jnp.where(low, uq, keys)
            packed = normed[c, 2 * RUN : 3 * RUN, :].astype(F32)
            qn = jnp.concatenate([packed, swap_halves(packed)], axis=0) * HEAD_DIM**0.5
            hat = jnp.where(low, qn, swap_halves(normed[c, 0 : 2 * RUN, :])) / gain
            factors = normed[c, 3 * RUN : 3 * RUN + 16, :].astype(F32)
            factors = factors[8:10, :] + factors[10:12, :]
            rows = jnp.concatenate(
                [factors, q_means[c : c + 1, :], k_means[c : c + 1, :], jnp.zeros((4, 128), F32)], axis=0
            )
            cols = jnp.transpose(jnp.concatenate([rows] * 16, axis=0))
            r = jnp.where(low, cols[:, 0:1], cols[:, 1:2])
            m = jnp.where(low, cols[:, 2:3], cols[:, 3:4])
            grad = r * (upstream * gain - hat * m)
            part = jnp.sum(upstream * hat, axis=0, keepdims=True)
            gains = part if gains is None else gains + part
            parts.append(jnp.where(low | (place[3] == 1), grad, both + other).astype(BF))
        left = jnp.concatenate([turned[2 * p], turned[2 * p + 1]], axis=1)
        step = dot(left, jnp.concatenate(parts, axis=0))
        total = step if total is None else total + step
    low_row = low[0:1, :]
    gains = jnp.where(low_row | (place[3] == 1), gains, 0.0)
    ffn = jnp.where(low_row, swap_halves(others[0:8, :])[0:1, :], 0.0)
    rows = jnp.concatenate([gains, ffn, jnp.zeros((6, 128), F32)], axis=0)
    some = lanes_of(8) < 64
    for s in range(8):
        out_ref[s, 0:128, :] = total[128 * s : 128 * (s + 1), :].astype(BF)
        kept = jnp.where(some, others[8 * (s // 2) : 8 * (s // 2) + 8, :], 0.0)
        out_ref[s, 128:144, :] = jnp.concatenate(
            [kept, rows if s == 0 else jnp.zeros((8, 128), F32)], axis=0
        ).astype(BF)
        out_ref[s, 144:PART, :] = jnp.zeros((64, 128), BF)
    for j in range(4):
        at = jnp.bitwise_xor(place[0], j % 2) * 4 + jnp.bitwise_xor(place[1], j // 2) * 2 + place[2]
        out_ref[pl.ds(at, 1), 144:PART, :] = out_rows[64 * j : 64 * j + 64, :].astype(BF)[None]


def head_grads(place, turned, own, kv_other, normed, grads, branch, gain):
    whole = lambda v: pl.BlockSpec(v.shape, lambda i: (0,) * v.ndim)
    n = own.shape[0]
    part = lambda rows, at: pl.BlockSpec((n, rows, 128), lambda i: (0, at // rows, 0))
    return pl.pallas_call(
        head_grad_kernel,
        grid=(1,),
        out_shape=like((8, PART, 128), BF),
        in_specs=[
            SM,
            whole(turned),
            part(RUN, BASE),
            part(RUN, BASE + RUN),
            part(RUN, BASE + 2 * RUN),
            whole(kv_other),
            whole(normed),
            part(BASE, 0),
            part(2 * n, BASE + 3 * RUN),
            part(EXPERTS, RUN),
            whole(gain),
        ],
        out_specs=pl.BlockSpec((8, PART, 128), lambda i: (0, 0, 0)),
        compiler_params=pltpu.CompilerParams(vmem_limit_bytes=62 * MIB),
        cost_estimate=pl.CostEstimate(
            flops=2 * 2048 * 1024 * 128, bytes_accessed=8 * 1024 * 1024, transcendentals=0
        ),
        name="head_grads",
    )(place, turned, own, own, own, kv_other, normed, grads, grads, branch, gain)


def share_kernel(shares, gain_ref, out_ref):
    total = shares[0].astype(F32)
    for s in range(1, shares.shape[0]):
        total = total + shares[s].astype(F32)
    total = jnp.concatenate([total[0:128], total[128:144] + gain_ref[...], total[144:PART]], axis=0)
    total = total.astype(BF)
    for c in range(out_ref.shape[0]):
        out_ref[c] = total


def share_out(shares, gain, chips):
    return call(
        share_kernel,
        like((chips, PART, 128), BF),
        [VM, VM],
        "share_out",
        1 << 18,
        4 * 1024 * 1024,
    )(shares, gain)


def spread_kernel(place, block_ref, *refs):
    wq, wk, wv, wo, router, x_gain, q_gain, k_gain, f_gain = refs[-9:]
    n = block_ref.shape[1]
    low = lanes_of(128) < 64
    some = lanes_of(8) < 64
    total = None
    kept = None
    queries, keys, seconds = [], [], []
    for c in range(0, n, 2):
        even, odd = block_ref[0, c, 0].astype(F32), block_ref[0, c + 1, 0].astype(F32)
        wide = slice(64 * c, 64 * c + 128)
        wq[0, 0, :, wide] = jnp.where(low, even[:128], swap_halves(odd[:128]))
        key, value = even[:128], odd[:128]
        if c % 4 == 0:
            kept = (swap_halves(key), swap_halves(value))
        else:
            half = slice(32 * c - 64, 32 * c + 64)
            wk[0, 0, :, half] = jnp.where(low, kept[0], key)
            wv[0, 0, :, half] = jnp.where(low, kept[1], value)
        router[:, wide] = jnp.where(some, even[128:136], swap_halves(odd[128:136]))
        sums = even[128:144] + odd[128:144]
        total = sums if total is None else total + sums
        pairs = jnp.where(some, even[136:144], swap_halves(odd[136:144]))
        queries.append(pairs[0:1])
        seconds.append(pairs[1:2])
        if c % 4 == 0:
            key_gain = swap_halves(even[136:144])
        else:
            keys.append(jnp.where(some, key_gain, even[136:144])[0:1])
        for d, block in ((c, even), (c + 1, odd)):
            for m in range(8):
                wo[0, 0, 8 * d : 8 * d + 8, 128 * m : 128 * (m + 1)] = block[144 + 8 * m : 152 + 8 * m]
    turned = swap_halves(total)
    firsts = [
        jnp.where(some[0:1], turned[2 * t : 2 * t + 1], total[2 * t + 1 : 2 * t + 2]) for t in range(4)
    ]
    firsts = jnp.concatenate(firsts + [total[10 + t : 11 + t] for t in range(4)], axis=1)

    @pl.when(pl.program_id(0) == 0)
    def _():
        ours = place[0] == 0
        given = refs[4:8] if len(refs) > 9 else None
        for i, (ref, made) in enumerate([(x_gain, None), (q_gain, queries), (k_gain, keys), (f_gain, seconds)]):
            old = jnp.zeros(ref.shape, F32) if given is None else given[i][...]
            ref[...] = old if made is None else jnp.where(ours, jnp.concatenate(made, axis=1), old)

    x_gain[...] += firsts


def spread(place, block, before=None):
    dp, n, y = block.shape[:3]
    steps = dp * y
    put = lambda rows, width: pl.BlockSpec((1, 1, rows, width), lambda i, at: (i, at[0], 0, 0))
    sizes = [(128, 1024), (128, 512), (128, 512), (128, 1024)]
    widths = [1024, 1024, 512, 1024]
    small = [pl.BlockSpec((1, w), lambda i, at: (0, 0)) for w in widths]
    given = () if before is None else tuple(before)
    return pl.pallas_call(
        spread_kernel,
        grid_spec=pltpu.PrefetchScalarGridSpec(
            num_scalar_prefetch=1,
            grid=(steps,),
            in_specs=[pl.BlockSpec((1, n, 1, PART, 128), lambda i, at: (i // y, 0, i % y, 0, 0))]
            + ([pl.BlockSpec(memory_space=pl.ANY)] * 4 + small if given else []),
            out_specs=[put(*size) for size in sizes]
            + [pl.BlockSpec((8, 1024), lambda i, at: (i, 0))]
            + small,
        ),
        out_shape=[like((steps, 2) + size, F32) for size in sizes]
        + [like((8 * steps, 1024), F32)]
        + [like((1, w), F32) for w in widths],
        input_output_aliases={2 + i: i for i in range(4 if given else 0)},
        compiler_params=pltpu.CompilerParams(vmem_limit_bytes=62 * MIB),
        name="spread",
    )(place, block, *given)


def by_ctx(value):
    return lax.all_to_all(value, "ctx", split_axis=0, concat_axis=0, tiled=True)


def swap(value, axis, bit):
    n = lax.axis_size(axis)
    return lax.ppermute(value, axis, [(i, i ^ bit) for i in range(n)])


def swap_y(value):
    n = lax.axis_size("dp") * lax.axis_size("exp")
    return lax.ppermute(value, ("dp", "exp"), [(i, i ^ 6) for i in range(n)])


def held(value):
    return lax.optimization_barrier(value)


def across_chips(value):
    axes = ("dp", "ctx", "exp")
    dp, ctx, exp = (lax.axis_size(a) for a in axes)
    groups = [
        [(d * ctx + c) * exp + 2 * y + core for d in range(dp) for c in range(ctx) for y in range(exp // 2)]
        for core in range(2)
    ]
    return lax.all_to_all(
        value, axes, split_axis=0, concat_axis=0, tiled=True, axis_index_groups=groups
    )


def per_device(
    tokens,
    places,
    choices,
    cotangent,
    attn_gain,
    w_query,
    w_key,
    w_value,
    query_gain,
    key_gain,
    w_out,
    ffn_gain,
    w_router,
    w_gate,
    w_up,
    w_down,
):
    x_low = tokens[0]
    rows = x_low.shape[0]
    ctx = lax.axis_index("ctx")
    exp = lax.axis_index("exp")
    n_ctx = lax.axis_size("ctx")
    n_dp = lax.axis_size("dp")
    core = jnp.bitwise_and(exp, 1).astype(jnp.int32)
    picked = choices[0]
    g_low = cotangent[0]

    inv = places[0, ::RUN] // RUN
    runs = jnp.arange(inv.shape[0], dtype=jnp.int32)
    order = jnp.sum(jnp.where(inv[None, :] == runs[:, None], runs[None, :], 0), axis=1)
    table = jnp.asarray(turn_tables(places.shape[1]))

    chosen = jnp.any(picked[:, :, None] == jnp.arange(EXPERTS, dtype=jnp.int32), axis=1)
    tri = jnp.asarray(np.tril(np.ones((rows, rows), np.float32), -1), BF)
    slot = dot(tri, chosen.astype(BF))
    slot = jnp.where(chosen, slot, -1.0).astype(BF)
    column = np.arange(EXPERTS * CAP)
    named = (np.arange(EXPERTS)[:, None] == (column // CAP)[None, :]).astype(np.float32)
    at = dot(slot, jnp.asarray(named, BF))
    spot = (at == jnp.asarray(column % CAP, F32)[None, :]).astype(BF)

    send, first_low, first_turned, q_proj, k_proj = pre(
        x_low, attn_gain, w_query, w_key, w_value, query_gain, key_gain, picked.T
    )
    g_all = lax.all_gather(g_low, "ctx")
    recv = by_ctx(send)
    recv, spot = held((recv, spot))
    kv_all, q_all, att_all, lse_all, att_send = attend(order, inv, recv, table)
    att_send, w_gate, w_up, w_down = held((att_send, w_gate, w_up, w_down))
    down_blocks = w_down.reshape(2, 128, 8, 128).transpose(0, 2, 1, 3).reshape(2, 1024, 128)
    mine = held(jnp.concatenate([w_gate, w_up, down_blocks], axis=1))
    over_y = swap_y(mine)
    over_core = swap(mine, "exp", 1)
    heads = by_ctx(att_send)
    heads, mine, first_turned = held((heads, mine, first_turned))
    turned_all = lax.all_gather(first_turned, "ctx")
    over_both = swap(over_y, "exp", 1)
    router = w_router.T
    attended, middle, second_low, rows_send = middle_forward(heads, x_low, w_out, ffn_gain, spot)
    sent = by_ctx(rows_send.reshape(n_ctx, 2, CAP, -1))
    number = jnp.reshape(2 * ctx, (1,)).astype(jnp.int32)
    g_rows, slots = cotangent_rows(number, recv, g_all)
    halves = attended.reshape(rows, 4, 2, 128)
    halves = lax.dynamic_index_in_dim(halves, 1 - core, axis=2, keepdims=False).reshape(rows, 512)
    halves = swap(halves, "exp", 1)
    sent, over_core, over_both, g_rows, halves = held((sent, over_core, over_both, g_rows, halves))
    parts = (mine, over_core, over_y, over_both)
    back = experts(number, sent, g_rows, router, parts)
    back = by_ctx(back).reshape(EXPERTS * CAP, -1)
    add = lambda *parts: sum(p.astype(F32) for p in parts).astype(BF)
    keep, near, far, out_part = weight_grads(number, sent, g_rows, router, slots, parts)
    back, near, keep, far, out_part, turned_all = held((back, near, keep, far, out_part, turned_all))
    out_part = lax.psum_scatter(out_part, "ctx", scatter_dimension=0, tiled=False)
    far = swap(far, "exp", 1)
    att_grad_send, grad_middle, branch = middle_back(
        spot, back, middle, second_low, router, ffn_gain, g_low, w_out
    )
    grad_recv = by_ctx(att_grad_send)
    even = 1 - jnp.bitwise_and(ctx, 1).astype(jnp.int32)
    place = jnp.stack([lax.axis_index("dp"), exp // 2, core, even]).astype(jnp.int32)
    begun = out_grads(place, attended, halves, branch, swap(branch, "exp", 1))
    near_a, near_b = (add(near[0, a], far[1, a]) for a in range(2))
    keep_a, keep_b = (add(keep[0, a], far[0, a]) for a in range(2))
    grad_recv, near_a, near_b, keep_a, keep_b, begun = held(
        (grad_recv, near_a, near_b, keep_a, keep_b, begun)
    )
    near_a = swap_y(near_a)
    near_b = swap_y(near_b)
    grad_send, kv_own = attend_back(
        order, inv, place[3:], grad_recv, kv_all, q_all, att_all, lse_all, table, begun
    )
    kv_other = swap(kv_own, "ctx", 1)
    grads = by_ctx(grad_send)
    keep_a = held(add(keep_a, near_a))
    dp_a = swap(keep_a, "dp", 1)
    keep_b = held(add(keep_b, near_b))
    dp_b = swap(keep_b, "dp", 1)
    grads, keep_a, keep_b, kv_other, dp_a = held((grads, keep_a, keep_b, kv_other, dp_a))
    own_gain = jnp.concatenate(
        [
            lax.dynamic_slice_in_dim(query_gain, ctx * HEAD_DIM, HEAD_DIM),
            lax.dynamic_slice_in_dim(key_gain, ctx // 2 * HEAD_DIM, HEAD_DIM),
        ]
    ).astype(F32)[None]
    shares = head_grads(
        place, turned_all, grad_send, kv_other, recv, grads, grad_recv, own_gain
    )
    shares, dp_b = held((shares, dp_b))
    shares = lax.all_to_all(shares, ("dp", "exp"), split_axis=0, concat_axis=0, tiled=True)
    input_grad, gain_part = input_back(
        grads, q_proj, k_proj, x_low, grad_middle, query_gain, key_gain, attn_gain, w_query, w_key, w_value
    )
    shares, gain_part, input_grad = held((shares, gain_part, input_grad))
    chips = n_dp * n_ctx * 2
    whole = across_chips(share_out(shares, gain_part, chips))
    sums = [k.astype(F32) + d.astype(F32) for k, d in ((keep_a, dp_a), (keep_b, dp_b))]
    grad_gate_w = jnp.stack([v[:1024] for v in sums])
    grad_up_w = jnp.stack([v[1024:2048] for v in sums])
    grad_down_w = jnp.stack(
        [v[2048:].reshape(8, 128, 128).transpose(1, 0, 2).reshape(128, 1024) for v in sums]
    )
    outputs = (middle + out_part.astype(F32)).astype(BF)
    whole, outputs, grad_gate_w, grad_up_w, grad_down_w = held(
        (whole, outputs, grad_gate_w, grad_up_w, grad_down_w)
    )
    other = swap(whole, "exp", 1)
    shape = (n_dp, n_ctx, 2, PART, 128)
    done = spread(jnp.reshape(core, (1,)), whole.reshape(shape))
    done = spread(jnp.reshape(1 - core, (1,)), other.reshape(shape), done[:4] + done[5:])
    wq, wk, wv, wo = (v.reshape(1024, -1) for v in done[:4])
    router_grad = done[4].T
    x_gain, q_gain, k_gain, f_gain = (v.reshape(-1) for v in done[5:])
    return (
        outputs[None],
        input_grad[None],
        x_gain,
        wq,
        wk,
        wv,
        q_gain,
        k_gain,
        wo,
        f_gain,
        router_grad,
        grad_gate_w,
        grad_up_w,
        grad_down_w,
    )


def solution(mesh):
    seqs = ("dp", "exp")
    row_spec = P(seqs, "ctx", None)
    in_specs = (row_spec, P(seqs, None), row_spec, row_spec) + (P(),) * 9
    in_specs += (P("ctx", None, "exp"), P("ctx", None, "exp"), P("ctx", "exp", None))
    out_specs = (row_spec, row_spec) + (P(),) * 9
    out_specs += (P("ctx", None, "exp"), P("ctx", None, "exp"), P("ctx", "exp", None))
    return jax.shard_map(
        per_device, mesh=mesh, in_specs=in_specs, out_specs=out_specs, check_vma=False
    )
```

profile of v0, /device:TPU:1, one launch (start us, length us, event | category | flops | bytes accessed | tf_op | source)
XLA Modules:
  0.0 350.7 jit_solution(16599914515267695393)
XLA Ops:
  12.2 8.6 %all-to-all-start = ((bf16[16,208,128]{2,1,0:T(8,128)(2,1)}), bf16[16,208,128]{2,1,0:T(8,128)(2,1)S(1)}, u32[]{:S(2)}, u32[]{:S(2)}) async-start(bf16[16,208,128]{2,1,0:T(8,128)(2,1)} %get-tuple-element.98), calls=%async_computation | async-start | bytes 1703936 | tf_op jit(solution)/shard_map/all_to_all | solution.py:882
  24.0 11.7 %all-to-all-done.recv.picks_ref.normed = bf16[16,208,128]{2,1,0:T(8,128)(2,1)S(1)} async-done(((bf16[16,208,128]{2,1,0:T(8,128)(2,1)}), bf16[16,208,128]{2,1,0:T(8,128)(2,1)S(1)}, u32[]{:S(2)}, u32[]{:S(2)}) %all-to-all-start) | async-done | bytes 852000 | tf_op jit(solution)/shard_map/all_to_all | solution.py:882
  36.6 7.2 %attend.1 = (bf16[2048,128]{1,0:T(8,128)(2,1)}, bf16[2048,128]{1,0:T(8,128)(2,1)}, bf16[2048,128]{1,0:T(8,128)(2,1)}, f32[8,2048]{1,0:T(8,128)}, bf16[16,64,128]{2,1,0:T(8,128)(2,1)}) custom-call(s32[32]{0:T(128)} %select_reduce_fusion.order, s32[32]{0:T(128)} %and_select_fusion.inv, bf16[16,208,128]{2,1,0:T(8,128)(2,1)} %copy-done.2, ...), custom_call_target="tpu_custom_call" | custom-call | flops 1073741824 | bytes 3670016 | tf_op jit(solution)/shard_map/attend/pallas_call | solution.py:214
  50.4 7.4 %all-to-all-done.1.heads = bf16[16,64,128]{2,1,0:T(8,128)(2,1)S(1)} async-done(((bf16[16,64,128]{2,1,0:T(8,128)(2,1)}), bf16[16,64,128]{2,1,0:T(8,128)(2,1)S(1)}, u32[]{:S(2)}, u32[]{:S(2)}) %all-to-all-start.1) | async-done | bytes 262176 | tf_op jit(solution)/shard_map/all_to_all | solution.py:882
  75.5 15.3 %collective-permute-done.1.refs_2_ = bf16[2,3072,128]{2,1,0:T(8,128)(2,1)} collective-permute-done((bf16[2,3072,128]{2,1,0:T(8,128)(2,1)}, bf16[2,3072,128]{2,1,0:T(8,128)(2,1)}, u32[]{:S(2)}, u32[]{:S(2)}) %collective-permute-start.1) | collective-permute-done | bytes 1572896 | tf_op jit(solution)/shard_map/ppermute | solution.py:892
  90.8 5.7 %collective-permute-start.2 = (bf16[2,3072,128]{2,1,0:T(8,128)(2,1)}, bf16[2,3072,128]{2,1,0:T(8,128)(2,1)}, u32[]{:S(2)}, u32[]{:S(2)}) collective-permute-start(bf16[2,3072,128]{2,1,0:T(8,128)(2,1)} %collective-permute-done.1.refs_2_), channel_id=1, source_target_pairs={{0,1},{1,0},{2,3},{3,2},{4,5},{5,4},{6,7},{7,6},{8,9},{9,8},{10,11... | collective-permute-start | bytes 4718600 | tf_op jit(solution)/shard_map/ppermute | solution.py:887
  97.9 5.6 %cotangent_rows.1 = (bf16[2,640,1024]{2,1,0:T(8,128)(2,1)}, f32[2,16,128]{2,1,0:T(8,128)}) custom-call(s32[1]{0:T(128)} %bitcast.4.number, bf16[16,208,128]{2,1,0:T(8,128)(2,1)} %copy-done.2, bf16[16,128,1024]{2,1,0:T(8,128)(2,1)} %all-gather.4.cloned.1.call-done.g_ref), custom_call_target="tpu_custom_call" | custom-call | flops 1342177280 | bytes 8388608 | tf_op jit(solution)/shard_map/cotangent_rows/pallas_call | solution.py:364
  103.5 13.9 %experts.1 = bf16[16,2,40,1152]{3,2,1,0:T(8,128)(2,1)} custom-call(s32[1]{0:T(128)} %bitcast.4.number, bf16[16,2,40,1024]{3,2,1,0:T(8,128)(2,1)} %all-to-all-done.2.rows_ref, bf16[2,640,1024]{2,1,0:T(8,128)(2,1)} %get-tuple-element.112.g_ref, bf16[32,1024]{1,0:T(8,128)(2,1)} %bitcast.99, bf16[2,3072,128]{2,1,0:T(8,128)(2,1)} %pad_maximum_fusion.refs_0_, ...), custom_call_target="tpu_custom_call" | custom-call | flops 8053063680 | bytes 20971520 | tf_op jit(solution)/shard_map/experts/pallas_call | solution.py:462
  117.4 5.5 %all-to-all-start.3 = ((bf16[16,2,40,1152]{3,2,1,0:T(8,128)(2,1)}), bf16[16,2,40,1152]{3,2,1,0:T(8,128)(2,1)}, u32[]{:S(2)}, u32[]{:S(2)}) async-start(bf16[16,2,40,1152]{3,2,1,0:T(8,128)(2,1)} %experts.1), calls=%async_computation.3 | async-start | bytes 5898240 | tf_op jit(solution)/shard_map/all_to_all | solution.py:882
  123.0 20.6 %weight_grads.1 = (bf16[1,2,3072,128]{3,2,1,0:T(8,128)(2,1)}, bf16[1,2,3072,128]{3,2,1,0:T(8,128)(2,1)}, bf16[2,2,3072,128]{3,2,1,0:T(8,128)(2,1)}, bf16[16,128,1024]{2,1,0:T(8,128)(2,1)}) custom-call(s32[1]{0:T(128)} %bitcast.4.number, bf16[16,2,40,1024]{3,2,1,0:T(8,128)(2,1)} %all-to-all-done.2.rows_ref, bf16[2,640,1024]{2,1,0:T(8,128)(2,1)} %get-tuple-element.112.g_ref, ...), custom_call_target="tpu_custom_call" | custom-call | flops 8053063680 | bytes 20971520 | tf_op jit(solution)/shard_map/weight_grads/pallas_call | solution.py:462
  143.6 14.7 %all-gather.6.cloned.1.call-done = bf16[16384,128]{1,0:T(8,128)(2,1)} async-done(((bf16[1024,128]{1,0:T(8,128)(2,1)}), bf16[16384,128]{1,0:T(8,128)(2,1)}) %all-gather.6.cloned.1.call-update) | async-done | bytes 4194320 | tf_op jit(solution)/shard_map/all_gather | solution.py:967
  158.3 9.9 %all-to-all-done.3 = bf16[16,2,40,1152]{3,2,1,0:T(8,128)(2,1)} async-done(((bf16[16,2,40,1152]{3,2,1,0:T(8,128)(2,1)}), bf16[16,2,40,1152]{3,2,1,0:T(8,128)(2,1)}, u32[]{:S(2)}, u32[]{:S(2)}) %all-to-all-start.3) | async-done | bytes 2949152 | tf_op jit(solution)/shard_map/all_to_all | solution.py:882
  168.2 6.3 %collective-permute-start.4 = (bf16[2,2,3072,128]{3,2,1,0:T(8,128)(2,1)}, bf16[2,2,3072,128]{3,2,1,0:T(8,128)(2,1)}, u32[]{:S(2)}, u32[]{:S(2)}) collective-permute-start(bf16[2,2,3072,128]{3,2,1,0:T(8,128)(2,1)} %get-tuple-element.128), channel_id=1, source_target_pairs={{0,1},{1,0},{2,3},{3,2},{4,5},{5,4},{6,7},{7,6},{8,9},{9,8},{10,11... | collective-permute-start | bytes 9437192 | tf_op jit(solution)/shard_map/ppermute | solution.py:887
  174.6 6.0 %middle_back.1 = (bf16[16,96,128]{2,1,0:T(8,128)(2,1)}, f32[128,1024]{1,0:T(8,128)}, bf16[128,1024]{1,0:T(8,128)(2,1)}) custom-call(bf16[128,1280]{1,0:T(8,128)(2,1)} %fusion.spot, bf16[1280,1152]{1,0:T(8,128)(2,1)} %bitcast.14.back, f32[128,1024]{1,0:T(8,128)} %get-tuple-element.124.middle_ref, bf16[128,1024]{1,0:T(8,128)(2,1)} %get-tuple-element.125.second, ...), custom_call_target="tpu_custom_call" | custom-call | flops 603979776 | bytes 6291456 | tf_op jit(solution)/shard_map/middle_back/pallas_call | solution.py:579
  197.8 8.7 %collective-permute-start.7 = (bf16[3072,128]{1,0:T(8,128)(2,1)}, bf16[3072,128]{1,0:T(8,128)(2,1)}, u32[]{:S(2)}, u32[]{:S(2)}) collective-permute-start(bf16[3072,128]{1,0:T(8,128)(2,1)} %get-tuple-element.142), channel_id=1, source_target_pairs={{0,66},{1,67},{2,64},{3,65},{64,2},{65,3},{66,0},{67,1},{4,70},{5,... | collective-permute-start | bytes 2359304 | tf_op jit(solution)/shard_map/ppermute | solution.py:892
  206.4 11.1 %attend_back.1 = (bf16[16,480,128]{2,1,0:T(8,128)(2,1)}, bf16[16,64,128]{2,1,0:T(8,128)(2,1)}) custom-call(s32[32]{0:T(128)} %select_reduce_fusion.order, s32[32]{0:T(128)} %and_select_fusion.inv, s32[1]{0:T(128)} %bitcast.3.even, bf16[16,96,128]{2,1,0:T(8,128)(2,1)} %copy-done.6, ...), custom_call_target="tpu_custom_call", output_to_operand_aliasing={{0}: (9, {})} | custom-call | flops 2684354560 | bytes 5242880 | tf_op jit(solution)/shard_map/attend_back/pallas_call | solution.py:306
  225.1 5.7 %collective-permute-done.7 = bf16[3072,128]{1,0:T(8,128)(2,1)} collective-permute-done((bf16[3072,128]{1,0:T(8,128)(2,1)}, bf16[3072,128]{1,0:T(8,128)(2,1)}, u32[]{:S(2)}, u32[]{:S(2)}) %collective-permute-start.7) | collective-permute-done | bytes 786464 | tf_op jit(solution)/shard_map/ppermute | solution.py:892
  235.3 18.1 %collective-permute-done.8.kv_other = bf16[16,64,128]{2,1,0:T(8,128)(2,1)S(1)} collective-permute-done((bf16[16,64,128]{2,1,0:T(8,128)(2,1)S(1)}, bf16[16,64,128]{2,1,0:T(8,128)(2,1)S(1)}, u32[]{:S(2)}, u32[]{:S(2)}) %collective-permute-start.8) | collective-permute-done | bytes 262176 | tf_op jit(solution)/shard_map/ppermute | solution.py:887
  254.1 6.7 %head_grads.1 = bf16[8,208,128]{2,1,0:T(8,128)(2,1)} custom-call(s32[4]{0:T(128)} %pad_add_fusion.place, bf16[16,1024,128]{2,1,0:T(8,128)(2,1)} %bitcast.83, bf16[16,480,128]{2,1,0:T(8,128)(2,1)} %get-tuple-element.138.early.later.queries, bf16[16,480,128]{2,1,0:T(8,128)(2,1)} %get-tuple-element.138.early.later.queries, ...), custom_call_target="tpu_custom_call" | custom-call | flops 536870912 | bytes 8388608 | tf_op jit(solution)/shard_map/head_grads/pallas_call | solution.py:757
  266.3 6.0 %input_back.1 = (f32[128,1024]{1,0:T(8,128)}, f32[16,128]{1,0:T(8,128)}) custom-call(bf16[16,480,128]{2,1,0:T(8,128)(2,1)} %all-to-all-done.5.out_parts.sums_ref.recv, f32[128,1024]{1,0:T(8,128)} %get-tuple-element.147.q_ref, f32[128,512]{1,0:T(8,128)} %get-tuple-element.148.k_ref, bf16[128,1024]{1,0:T(8,128)(2,1)} %bitcast.89, ...), custom_call_target="tpu_custom_call" | custom-call | flops 536870912 | bytes 8388608 | tf_op jit(solution)/shard_map/input_back/pallas_call | solution.py:680
  277.9 8.8 %all-to-all-start.7 = ((bf16[64,208,128]{2,1,0:T(8,128)(2,1)}), bf16[64,208,128]{2,1,0:T(8,128)(2,1)}, u32[]{:S(2)}, u32[]{:S(2)}) async-start(bf16[64,208,128]{2,1,0:T(8,128)(2,1)} %share_out.1), calls=%async_computation.7 | async-start | bytes 6815744 | tf_op jit(solution)/shard_map/all_to_all | solution.py:906
  297.5 30.6 %all-to-all-done.7 = bf16[64,208,128]{2,1,0:T(8,128)(2,1)} async-done(((bf16[64,208,128]{2,1,0:T(8,128)(2,1)}), bf16[64,208,128]{2,1,0:T(8,128)(2,1)}, u32[]{:S(2)}, u32[]{:S(2)}) %all-to-all-start.7) | async-done | bytes 3407904 | tf_op jit(solution)/shard_map/all_to_all | solution.py:906
  332.4 5.4 %spread.2 = (f32[4,2,128,1024]{3,2,1,0:T(8,128)}, f32[4,2,128,512]{3,2,1,0:T(8,128)}, f32[4,2,128,512]{3,2,1,0:T(8,128)}, f32[4,2,128,1024]{3,2,1,0:T(8,128)}, f...) custom-call(s32[1]{0:T(128)} %bitcast.2.place, ...), custom_call_target="tpu_custom_call" | custom-call | tf_op jit(solution)/shard_map/spread/pallas_call | solution.py:861
  338.4 5.6 %spread.3 = (f32[4,2,128,1024]{3,2,1,0:T(8,128)}, f32[4,2,128,512]{3,2,1,0:T(8,128)}, f32[4,2,128,512]{3,2,1,0:T(8,128)}, f32[4,2,128,1024]{3,2,1,0:T(8,128)}, f...) custom-call(s32[1]{0:T(128)} %bitcast.34.place, ...), custom_call_target="tpu_custom_call", output_to_operand_aliasing={{0}: (2, {}), {1}: (3, {}), {2}: (4, {}), {3}: (5, {})} | custom-call | tf_op jit(solution)/shard_map/spread/pallas_call | solution.py:861
  (108 shorter events, 91.1 us)
Async XLA Ops:
  7.2 41.8 %copy-start = (bf16[2,128,1024]{2,1,0:T(8,128)(2,1)S(1)}, bf16[2,128,1024]{2,1,0:T(8,128)(2,1)}, u32[]{:S(2)}) copy-start(bf16[2,128,1024]{2,1,0:T(8,128)(2,1)} %param.35) | copy-start | bytes 1572868
  7.2 90.7 %all-gather.4.cloned.1.call-start = ((), (), s32[]{:S(2)}) async-start(), calls=%async_computation.9 | async-start | bytes 4456448 | tf_op jit(solution)/shard_map/all_gather | solution.py:956
  12.2 23.5 %all-to-all-start = ((bf16[16,208,128]{2,1,0:T(8,128)(2,1)}), bf16[16,208,128]{2,1,0:T(8,128)(2,1)S(1)}, u32[]{:S(2)}, u32[]{:S(2)}) async-start(bf16[16,208,128]{2,1,0:T(8,128)(2,1)} %get-tuple-element.98), calls=%async_computation | async-start | bytes 1703936 | tf_op jit(solution)/shard_map/all_to_all | solution.py:882
  43.9 13.9 %all-to-all-start.1 = ((bf16[16,64,128]{2,1,0:T(8,128)(2,1)}), bf16[16,64,128]{2,1,0:T(8,128)(2,1)S(1)}, u32[]{:S(2)}, u32[]{:S(2)}) async-start(bf16[16,64,128]{2,1,0:T(8,128)(2,1)} %get-tuple-element.101), calls=%async_computation.1 | async-start | bytes 524288 | tf_op jit(solution)/shard_map/all_to_all | solution.py:882
  48.9 109.3 %all-gather.6.cloned.1.call-start = ((), (), s32[]{:S(2)}) async-start(), calls=%async_computation.10 | async-start | bytes 4456448 | tf_op jit(solution)/shard_map/all_gather | solution.py:967
  57.8 33.0 %collective-permute-start.1 = (bf16[2,3072,128]{2,1,0:T(8,128)(2,1)}, bf16[2,3072,128]{2,1,0:T(8,128)(2,1)}, u32[]{:S(2)}, u32[]{:S(2)}) collective-permute-start(bf16[2,3072,128]{2,1,0:T(8,128)(2,1)} %pad_maximum_fusion.refs_0_), channel_id=1, source_target_pairs={{0,66},{1,67},{2,64},{3,65},{64,2},{65,3},{66,0},{67,1},{4,70},{5,... | collective-permute-start | bytes 4718600 | tf_op jit(solution)/shard_map/ppermute | solution.py:892
  65.6 37.9 %all-to-all-start.2 = ((bf16[16,2,40,1024]{3,2,1,0:T(8,128)(2,1)}), bf16[16,2,40,1024]{3,2,1,0:T(8,128)(2,1)}, u32[]{:S(2)}, u32[]{:S(2)}) async-start(bf16[16,2,40,1024]{3,2,1,0:T(8,128)(2,1)} %bitcast.86), calls=%async_computation.2 | async-start | bytes 5242880 | tf_op jit(solution)/shard_map/all_to_all | solution.py:882
  70.3 33.1 %collective-permute-start = (bf16[2,3072,128]{2,1,0:T(8,128)(2,1)}, bf16[2,3072,128]{2,1,0:T(8,128)(2,1)}, u32[]{:S(2)}, u32[]{:S(2)}) collective-permute-start(bf16[2,3072,128]{2,1,0:T(8,128)(2,1)} %pad_maximum_fusion.refs_0_), channel_id=1, source_target_pairs={{0,1},{1,0},{2,3},{3,2},{4,5},{5,4},{6,7},{7,6},{8,9},{9,8},{10,11... | collective-permute-start | bytes 4718600 | tf_op jit(solution)/shard_map/ppermute | solution.py:887
  90.8 12.7 %collective-permute-start.2 = (bf16[2,3072,128]{2,1,0:T(8,128)(2,1)}, bf16[2,3072,128]{2,1,0:T(8,128)(2,1)}, u32[]{:S(2)}, u32[]{:S(2)}) collective-permute-start(bf16[2,3072,128]{2,1,0:T(8,128)(2,1)} %collective-permute-done.1.refs_2_), channel_id=1, source_target_pairs={{0,1},{1,0},{2,3},{3,2},{4,5},{5,4},{6,7},{7,6},{8,9},{9,8},{10,11... | collective-permute-start | bytes 4718600 | tf_op jit(solution)/shard_map/ppermute | solution.py:887
  97.5 5.9 %collective-permute-start.3 = (bf16[128,512]{1,0:T(8,128)(2,1)S(1)}, bf16[128,512]{1,0:T(8,128)(2,1)S(1)}, u32[]{:S(2)}, u32[]{:S(2)}) collective-permute-start(bf16[128,512]{1,0:T(8,128)(2,1)S(1)} %bitcast.98), channel_id=1, source_target_pairs={{0,1},{1,0},{2,3},{3,2},{4,5},{5,4},{6,7},{7,6},{8,9},{9,8},{10,11... | collective-permute-start | bytes 393224 | tf_op jit(solution)/shard_map/ppermute | solution.py:887
  117.4 50.8 %all-to-all-start.3 = ((bf16[16,2,40,1152]{3,2,1,0:T(8,128)(2,1)}), bf16[16,2,40,1152]{3,2,1,0:T(8,128)(2,1)}, u32[]{:S(2)}, u32[]{:S(2)}) async-start(bf16[16,2,40,1152]{3,2,1,0:T(8,128)(2,1)} %experts.1), calls=%async_computation.3 | async-start | bytes 5898240 | tf_op jit(solution)/shard_map/all_to_all | solution.py:882
  122.9 172.7 %reduce-scatter.4.cloned.1.call-start = ((), (), s32[]{:S(2)}) async-start(), calls=%async_computation.11 | async-start | bytes 4456448
  168.2 20.2 %collective-permute-start.4 = (bf16[2,2,3072,128]{3,2,1,0:T(8,128)(2,1)}, bf16[2,2,3072,128]{3,2,1,0:T(8,128)(2,1)}, u32[]{:S(2)}, u32[]{:S(2)}) collective-permute-start(bf16[2,2,3072,128]{3,2,1,0:T(8,128)(2,1)} %get-tuple-element.128), channel_id=1, source_target_pairs={{0,1},{1,0},{2,3},{3,2},{4,5},{5,4},{6,7},{7,6},{8,9},{9,8},{10,11... | collective-permute-start | bytes 9437192 | tf_op jit(solution)/shard_map/ppermute | solution.py:887
  180.5 4.3 %collective-permute-start.5 = (bf16[128,1024]{1,0:T(8,128)(2,1)}, bf16[128,1024]{1,0:T(8,128)(2,1)S(1)}, u32[]{:S(2)}, u32[]{:S(2)}) collective-permute-start(bf16[128,1024]{1,0:T(8,128)(2,1)} %get-tuple-element.131.branch), channel_id=1, source_target_pairs={{0,1},{1,0},{2,3},{3,2},{4,5},{5,4},{6,7},{7,6},{8,9},{9,8},{10,11... | collective-permute-start | bytes 786440 | tf_op jit(solution)/shard_map/ppermute | solution.py:887
  181.1 14.1 %all-to-all-start.4 = ((bf16[16,96,128]{2,1,0:T(8,128)(2,1)}), bf16[16,96,128]{2,1,0:T(8,128)(2,1)S(1)}, u32[]{:S(2)}, u32[]{:S(2)}) async-start(bf16[16,96,128]{2,1,0:T(8,128)(2,1)} %get-tuple-element.126), calls=%async_computation.4 | async-start | bytes 786432 | tf_op jit(solution)/shard_map/all_to_all | solution.py:882
  195.3 27.6 %collective-permute-start.6 = (bf16[3072,128]{1,0:T(8,128)(2,1)}, bf16[3072,128]{1,0:T(8,128)(2,1)}, u32[]{:S(2)}, u32[]{:S(2)}) collective-permute-start(bf16[3072,128]{1,0:T(8,128)(2,1)} %get-tuple-element.140), channel_id=1, source_target_pairs={{0,66},{1,67},{2,64},{3,65},{64,2},{65,3},{66,0},{67,1},{4,70},{5,... | collective-permute-start | bytes 2359304 | tf_op jit(solution)/shard_map/ppermute | solution.py:892
  197.8 33.1 %collective-permute-start.7 = (bf16[3072,128]{1,0:T(8,128)(2,1)}, bf16[3072,128]{1,0:T(8,128)(2,1)}, u32[]{:S(2)}, u32[]{:S(2)}) collective-permute-start(bf16[3072,128]{1,0:T(8,128)(2,1)} %get-tuple-element.142), channel_id=1, source_target_pairs={{0,66},{1,67},{2,64},{3,65},{64,2},{65,3},{66,0},{67,1},{4,70},{5,... | collective-permute-start | bytes 2359304 | tf_op jit(solution)/shard_map/ppermute | solution.py:892
  217.5 35.9 %all-to-all-start.5 = ((bf16[16,480,128]{2,1,0:T(8,128)(2,1)}), bf16[16,480,128]{2,1,0:T(8,128)(2,1)}, u32[]{:S(2)}, u32[]{:S(2)}) async-start(bf16[16,480,128]{2,1,0:T(8,128)(2,1)} %get-tuple-element.138.early.later.queries), calls=%async_computation.5 | async-start | bytes 3932160 | tf_op jit(solution)/shard_map/all_to_all | solution.py:882
  225.1 28.3 %collective-permute-start.9 = (bf16[3072,128]{1,0:T(8,128)(2,1)}, bf16[3072,128]{1,0:T(8,128)(2,1)}, u32[]{:S(2)}, u32[]{:S(2)}) collective-permute-start(bf16[3072,128]{1,0:T(8,128)(2,1)} %add_convert_fusion.1), channel_id=1, source_target_pairs={{0,64},{64,0},{1,65},{65,1},{2,66},{66,2},{3,67},{67,3},{4,68},{68... | collective-permute-start | bytes 2359304 | tf_op jit(solution)/shard_map/ppermute | solution.py:887
  233.1 27.8 %collective-permute-start.10 = (bf16[3072,128]{1,0:T(8,128)(2,1)}, bf16[3072,128]{1,0:T(8,128)(2,1)S(1)}, u32[]{:S(2)}, u32[]{:S(2)}) collective-permute-start(bf16[3072,128]{1,0:T(8,128)(2,1)} %add_convert_fusion), channel_id=1, source_target_pairs={{0,64},{64,0},{1,65},{65,1},{2,66},{66,2},{3,67},{67,3},{4,68},{68... | collective-permute-start | bytes 2359304 | tf_op jit(solution)/shard_map/ppermute | solution.py:887
  233.1 20.3 %collective-permute-start.8 = (bf16[16,64,128]{2,1,0:T(8,128)(2,1)S(1)}, bf16[16,64,128]{2,1,0:T(8,128)(2,1)S(1)}, u32[]{:S(2)}, u32[]{:S(2)}) collective-permute-start(bf16[16,64,128]{2,1,0:T(8,128)(2,1)S(1)} %copy-done.19), channel_id=1, source_target_pairs={{0,4},{4,0},{8,12},{12,8},{16,20},{20,16},{24,28},{28,24},{32,36},... | collective-permute-start | bytes 786440 | tf_op jit(solution)/shard_map/ppermute | solution.py:887
  260.9 13.3 %all-to-all-start.6 = ((bf16[8,208,128]{2,1,0:T(8,128)(2,1)}), bf16[8,208,128]{2,1,0:T(8,128)(2,1)S(1)}, u32[]{:S(2)}, u32[]{:S(2)}) async-start(bf16[8,208,128]{2,1,0:T(8,128)(2,1)} %head_grads.1), calls=%async_computation.6 | async-start | bytes 851968 | tf_op jit(solution)/shard_map/all_to_all | solution.py:1020
  277.9 50.2 %all-to-all-start.7 = ((bf16[64,208,128]{2,1,0:T(8,128)(2,1)}), bf16[64,208,128]{2,1,0:T(8,128)(2,1)}, u32[]{:S(2)}, u32[]{:S(2)}) async-start(bf16[64,208,128]{2,1,0:T(8,128)(2,1)} %share_out.1), calls=%async_computation.7 | async-start | bytes 6815744 | tf_op jit(solution)/shard_map/all_to_all | solution.py:906
  328.1 10.3 %collective-permute-start.11 = (bf16[64,208,128]{2,1,0:T(8,128)(2,1)}, bf16[64,208,128]{2,1,0:T(8,128)(2,1)}, u32[]{:S(2)}, u32[]{:S(2)}) collective-permute-start(bf16[64,208,128]{2,1,0:T(8,128)(2,1)} %all-to-all-done.7), channel_id=1, source_target_pairs={{0,1},{1,0},{2,3},{3,2},{4,5},{5,4},{6,7},{7,6},{8,9},{9,8},{10,11... | collective-permute-start | bytes 10223624 | tf_op jit(solution)/shard_map/ppermute | solution.py:887
  (19 other events, 143.5 us)
Sparse Core Ops, SparseCore 0:
  10.2 61.9 all-gather.3
  74.9 83.3 all-gather.5
  174.7 90.9 reduce-scatter.3
where the time goes:
time: 357 us; the launch traced here: 351 us
  waiting for transfers between devices  119 us (33%)
  Pallas kernels  103 us (29%)
  starting transfers between devices  84.1 us (24%)
  other arithmetic  21.5 us (6%)
  between operations  14.3 us (4%)
  local copies, waits for them, and re-layouts  7.75 us (2%)
    pallas_call x2, Pallas kernels, expert_call(): pl.pallas_call(kernel, grid=(2,), out_shape=outs, in_specs=[SM, pl.BlockS...  34.5 us
    all_to_all x6, starting transfers between devices, by_ctx(): return lax.all_to_all(value, 'ctx', split_axis=0, concat_axis=0, tiled=True)  32.9 us
    all_to_all x6, waiting for transfers between devices, by_ctx(): return lax.all_to_all(value, 'ctx', split_axis=0, concat_axis=0, tiled=True)  31.2 us
    all_to_all x1, waiting for transfers between devices, across_chips(): lax.all_to_all(value, axes, split_axis=0, concat_axis=0, tiled=True, axis...  30.6 us
    ppermute x9, starting transfers between devices, swap(): return lax.ppermute(value, axis, [(i, i ^ bit) for i in range(n)])  22.7 us
    ppermute x3, waiting for transfers between devices, swap_y(): return lax.ppermute(value, ('dp', 'exp'), [(i, i ^ 6) for i in range(n)])  21.1 us
    ppermute x9, waiting for transfers between devices, swap(): return lax.ppermute(value, axis, [(i, i ^ bit) for i in range(n)])  18.7 us
    all_gather x1, waiting for transfers between devices, per_device(): turned_all = lax.all_gather(first_turned, 'ctx')  14.7 us
  transfers between devices with their start and end apart: 23, of which 11 were waited for; matrix products, arithmetic and copies ran while one was open for 8% of the time, Pallas kernels for 28%

commit v1 on v0

--- a/solution.py
+++ b/solution.py
@@ -989,7 +989,8 @@
     grad_recv = by_ctx(att_grad_send)
     even = 1 - jnp.bitwise_and(ctx, 1).astype(jnp.int32)
     place = jnp.stack([lax.axis_index("dp"), exp // 2, core, even]).astype(jnp.int32)
-    begun = out_grads(place, attended, halves, branch, swap(branch, "exp", 1))
+    other_branch = swap(grad_middle.astype(BF), "exp", 1)
+    begun = out_grads(place, attended, halves, branch, other_branch)
     near_a, near_b = (add(near[0, a], far[1, a]) for a in range(2))
     keep_a, keep_b = (add(keep[0, a], far[0, a]) for a in range(2))
     grad_recv, near_a, near_b, keep_a, keep_b, begun = held(

time: 357 us -> 358 us (level)
  no operation moved by 1% of the time
where the time goes in v1:
time: 358 us; the launch traced here: 352 us
  waiting for transfers between devices  119 us (33%)
  Pallas kernels  103 us (29%)
  starting transfers between devices  84.3 us (24%)
  other arithmetic  22.6 us (6%)
  between operations  14.4 us (4%)
  local copies, waits for them, and re-layouts  7.75 us (2%)
    pallas_call x2, Pallas kernels, expert_call(): pl.pallas_call(kernel, grid=(2,), out_shape=outs, in_specs=[SM, pl.BlockS...  34.6 us
    all_to_all x6, starting transfers between devices, by_ctx(): return lax.all_to_all(value, 'ctx', split_axis=0, concat_axis=0, tiled=True)  33.3 us
    all_to_all x1, waiting for transfers between devices, across_chips(): lax.all_to_all(value, axes, split_axis=0, concat_axis=0, tiled=True, axis...  30.6 us
    all_to_all x6, waiting for transfers between devices, by_ctx(): return lax.all_to_all(value, 'ctx', split_axis=0, concat_axis=0, tiled=True)  30.4 us
    ppermute x9, starting transfers between devices, swap(): return lax.ppermute(value, axis, [(i, i ^ bit) for i in range(n)])  22.6 us
    ppermute x9, waiting for transfers between devices, swap(): return lax.ppermute(value, axis, [(i, i ^ bit) for i in range(n)])  20.4 us
    ppermute x3, waiting for transfers between devices, swap_y(): return lax.ppermute(value, ('dp', 'exp'), [(i, i ^ 6) for i in range(n)])  20.1 us
    ppermute x3, starting transfers between devices, swap_y(): return lax.ppermute(value, ('dp', 'exp'), [(i, i ^ 6) for i in range(n)])  14.6 us
  transfers between devices with their start and end apart: 23, of which 11 were waited for; matrix products, arithmetic and copies ran while one was open for 8% of the time, Pallas kernels for 28%

profile of v1, /device:TPU:1, one launch (start us, length us, event | category | flops | bytes accessed | tf_op | source)
XLA Modules:
  0.0 352.1 jit_solution(11876410962587765598)
XLA Ops:
  12.2 8.6 %all-to-all-start = ((bf16[16,208,128]{2,1,0:T(8,128)(2,1)}), bf16[16,208,128]{2,1,0:T(8,128)(2,1)S(1)}, u32[]{:S(2)}, u32[]{:S(2)}) async-start(bf16[16,208,128]{2,1,0:T(8,128)(2,1)} %get-tuple-element.98), calls=%async_computation | async-start | bytes 1703936 | tf_op jit(solution)/shard_map/all_to_all | solution.py:882
  24.0 11.7 %all-to-all-done.recv.picks_ref.normed = bf16[16,208,128]{2,1,0:T(8,128)(2,1)S(1)} async-done(((bf16[16,208,128]{2,1,0:T(8,128)(2,1)}), bf16[16,208,128]{2,1,0:T(8,128)(2,1)S(1)}, u32[]{:S(2)}, u32[]{:S(2)}) %all-to-all-start) | async-done | bytes 852000 | tf_op jit(solution)/shard_map/all_to_all | solution.py:882
  36.6 7.2 %attend.1 = (bf16[2048,128]{1,0:T(8,128)(2,1)}, bf16[2048,128]{1,0:T(8,128)(2,1)}, bf16[2048,128]{1,0:T(8,128)(2,1)}, f32[8,2048]{1,0:T(8,128)}, bf16[16,64,128]{2,1,0:T(8,128)(2,1)}) custom-call(s32[32]{0:T(128)} %select_reduce_fusion.order, s32[32]{0:T(128)} %and_select_fusion.inv, bf16[16,208,128]{2,1,0:T(8,128)(2,1)} %copy-done.2, ...), custom_call_target="tpu_custom_call" | custom-call | flops 1073741824 | bytes 3670016 | tf_op jit(solution)/shard_map/attend/pallas_call | solution.py:214
  50.4 7.4 %all-to-all-done.1.heads = bf16[16,64,128]{2,1,0:T(8,128)(2,1)S(1)} async-done(((bf16[16,64,128]{2,1,0:T(8,128)(2,1)}), bf16[16,64,128]{2,1,0:T(8,128)(2,1)S(1)}, u32[]{:S(2)}, u32[]{:S(2)}) %all-to-all-start.1) | async-done | bytes 262176 | tf_op jit(solution)/shard_map/all_to_all | solution.py:882
  75.5 15.3 %collective-permute-done.1.refs_2_ = bf16[2,3072,128]{2,1,0:T(8,128)(2,1)} collective-permute-done((bf16[2,3072,128]{2,1,0:T(8,128)(2,1)}, bf16[2,3072,128]{2,1,0:T(8,128)(2,1)}, u32[]{:S(2)}, u32[]{:S(2)}) %collective-permute-start.1) | collective-permute-done | bytes 1572896 | tf_op jit(solution)/shard_map/ppermute | solution.py:892
  90.9 5.7 %collective-permute-start.2 = (bf16[2,3072,128]{2,1,0:T(8,128)(2,1)}, bf16[2,3072,128]{2,1,0:T(8,128)(2,1)}, u32[]{:S(2)}, u32[]{:S(2)}) collective-permute-start(bf16[2,3072,128]{2,1,0:T(8,128)(2,1)} %collective-permute-done.1.refs_2_), channel_id=1, source_target_pairs={{0,1},{1,0},{2,3},{3,2},{4,5},{5,4},{6,7},{7,6},{8,9},{9,8},{10,11... | collective-permute-start | bytes 4718600 | tf_op jit(solution)/shard_map/ppermute | solution.py:887
  97.9 5.6 %cotangent_rows.1 = (bf16[2,640,1024]{2,1,0:T(8,128)(2,1)}, f32[2,16,128]{2,1,0:T(8,128)}) custom-call(s32[1]{0:T(128)} %bitcast.4.number, bf16[16,208,128]{2,1,0:T(8,128)(2,1)} %copy-done.2, bf16[16,128,1024]{2,1,0:T(8,128)(2,1)} %all-gather.4.cloned.1.call-done.g_ref), custom_call_target="tpu_custom_call" | custom-call | flops 1342177280 | bytes 8388608 | tf_op jit(solution)/shard_map/cotangent_rows/pallas_call | solution.py:364
  103.5 13.9 %experts.1 = bf16[16,2,40,1152]{3,2,1,0:T(8,128)(2,1)} custom-call(s32[1]{0:T(128)} %bitcast.4.number, bf16[16,2,40,1024]{3,2,1,0:T(8,128)(2,1)} %all-to-all-done.2.rows_ref, bf16[2,640,1024]{2,1,0:T(8,128)(2,1)} %get-tuple-element.112.g_ref, bf16[32,1024]{1,0:T(8,128)(2,1)} %bitcast.99, bf16[2,3072,128]{2,1,0:T(8,128)(2,1)} %pad_maximum_fusion.refs_0_, ...), custom_call_target="tpu_custom_call" | custom-call | flops 8053063680 | bytes 20971520 | tf_op jit(solution)/shard_map/experts/pallas_call | solution.py:462
  117.5 5.5 %all-to-all-start.3 = ((bf16[16,2,40,1152]{3,2,1,0:T(8,128)(2,1)}), bf16[16,2,40,1152]{3,2,1,0:T(8,128)(2,1)}, u32[]{:S(2)}, u32[]{:S(2)}) async-start(bf16[16,2,40,1152]{3,2,1,0:T(8,128)(2,1)} %experts.1), calls=%async_computation.3 | async-start | bytes 5898240 | tf_op jit(solution)/shard_map/all_to_all | solution.py:882
  123.0 20.6 %weight_grads.1 = (bf16[1,2,3072,128]{3,2,1,0:T(8,128)(2,1)}, bf16[1,2,3072,128]{3,2,1,0:T(8,128)(2,1)}, bf16[2,2,3072,128]{3,2,1,0:T(8,128)(2,1)}, bf16[16,128,1024]{2,1,0:T(8,128)(2,1)}) custom-call(s32[1]{0:T(128)} %bitcast.4.number, bf16[16,2,40,1024]{3,2,1,0:T(8,128)(2,1)} %all-to-all-done.2.rows_ref, bf16[2,640,1024]{2,1,0:T(8,128)(2,1)} %get-tuple-element.112.g_ref, ...), custom_call_target="tpu_custom_call" | custom-call | flops 8053063680 | bytes 20971520 | tf_op jit(solution)/shard_map/weight_grads/pallas_call | solution.py:462
  143.6 14.6 %all-gather.6.cloned.1.call-done = bf16[16384,128]{1,0:T(8,128)(2,1)} async-done(((bf16[1024,128]{1,0:T(8,128)(2,1)}), bf16[16384,128]{1,0:T(8,128)(2,1)}) %all-gather.6.cloned.1.call-update) | async-done | bytes 4194320 | tf_op jit(solution)/shard_map/all_gather | solution.py:967
  158.2 10.0 %all-to-all-done.3 = bf16[16,2,40,1152]{3,2,1,0:T(8,128)(2,1)} async-done(((bf16[16,2,40,1152]{3,2,1,0:T(8,128)(2,1)}), bf16[16,2,40,1152]{3,2,1,0:T(8,128)(2,1)}, u32[]{:S(2)}, u32[]{:S(2)}) %all-to-all-start.3) | async-done | bytes 2949152 | tf_op jit(solution)/shard_map/all_to_all | solution.py:882
  168.2 6.3 %collective-permute-start.4 = (bf16[2,2,3072,128]{3,2,1,0:T(8,128)(2,1)}, bf16[2,2,3072,128]{3,2,1,0:T(8,128)(2,1)}, u32[]{:S(2)}, u32[]{:S(2)}) collective-permute-start(bf16[2,2,3072,128]{3,2,1,0:T(8,128)(2,1)} %get-tuple-element.128), channel_id=1, source_target_pairs={{0,1},{1,0},{2,3},{3,2},{4,5},{5,4},{6,7},{7,6},{8,9},{9,8},{10,11... | collective-permute-start | bytes 9437192 | tf_op jit(solution)/shard_map/ppermute | solution.py:887
  174.6 6.0 %middle_back.1 = (bf16[16,96,128]{2,1,0:T(8,128)(2,1)}, f32[128,1024]{1,0:T(8,128)}, bf16[128,1024]{1,0:T(8,128)(2,1)}) custom-call(bf16[128,1280]{1,0:T(8,128)(2,1)} %fusion.spot, bf16[1280,1152]{1,0:T(8,128)(2,1)} %bitcast.14.back, f32[128,1024]{1,0:T(8,128)} %get-tuple-element.124.middle_ref, bf16[128,1024]{1,0:T(8,128)(2,1)} %get-tuple-element.125.second, ...), custom_call_target="tpu_custom_call" | custom-call | flops 603979776 | bytes 6291456 | tf_op jit(solution)/shard_map/middle_back/pallas_call | solution.py:579
  198.8 8.5 %collective-permute-start.7 = (bf16[3072,128]{1,0:T(8,128)(2,1)}, bf16[3072,128]{1,0:T(8,128)(2,1)}, u32[]{:S(2)}, u32[]{:S(2)}) collective-permute-start(bf16[3072,128]{1,0:T(8,128)(2,1)} %get-tuple-element.143), channel_id=1, source_target_pairs={{0,66},{1,67},{2,64},{3,65},{64,2},{65,3},{66,0},{67,1},{4,70},{5,... | collective-permute-start | bytes 2359304 | tf_op jit(solution)/shard_map/ppermute | solution.py:892
  207.3 11.1 %attend_back.1 = (bf16[16,480,128]{2,1,0:T(8,128)(2,1)}, bf16[16,64,128]{2,1,0:T(8,128)(2,1)}) custom-call(s32[32]{0:T(128)} %select_reduce_fusion.order, s32[32]{0:T(128)} %and_select_fusion.inv, s32[1]{0:T(128)} %bitcast.3.even, bf16[16,96,128]{2,1,0:T(8,128)(2,1)} %copy-done.6, ...), custom_call_target="tpu_custom_call", output_to_operand_aliasing={{0}: (9, {})} | custom-call | flops 2684354560 | bytes 5242880 | tf_op jit(solution)/shard_map/attend_back/pallas_call | solution.py:306
  218.4 5.8 %all-to-all-start.5 = ((bf16[16,480,128]{2,1,0:T(8,128)(2,1)}), bf16[16,480,128]{2,1,0:T(8,128)(2,1)}, u32[]{:S(2)}, u32[]{:S(2)}) async-start(bf16[16,480,128]{2,1,0:T(8,128)(2,1)} %get-tuple-element.139.early.later.queries), calls=%async_computation.5 | async-start | bytes 3932160 | tf_op jit(solution)/shard_map/all_to_all | solution.py:882
  235.5 19.8 %collective-permute-done.8.kv_other = bf16[16,64,128]{2,1,0:T(8,128)(2,1)S(1)} collective-permute-done((bf16[16,64,128]{2,1,0:T(8,128)(2,1)S(1)}, bf16[16,64,128]{2,1,0:T(8,128)(2,1)S(1)}, u32[]{:S(2)}, u32[]{:S(2)}) %collective-permute-start.8) | collective-permute-done | bytes 262176 | tf_op jit(solution)/shard_map/ppermute | solution.py:887
  256.0 6.8 %head_grads.1 = bf16[8,208,128]{2,1,0:T(8,128)(2,1)} custom-call(s32[4]{0:T(128)} %pad_add_fusion.place, bf16[16,1024,128]{2,1,0:T(8,128)(2,1)} %bitcast.83, bf16[16,480,128]{2,1,0:T(8,128)(2,1)} %get-tuple-element.139.early.later.queries, bf16[16,480,128]{2,1,0:T(8,128)(2,1)} %get-tuple-element.139.early.later.queries, ...), custom_call_target="tpu_custom_call" | custom-call | flops 536870912 | bytes 8388608 | tf_op jit(solution)/shard_map/head_grads/pallas_call | solution.py:757
  267.8 6.0 %input_back.1 = (f32[128,1024]{1,0:T(8,128)}, f32[16,128]{1,0:T(8,128)}) custom-call(bf16[16,480,128]{2,1,0:T(8,128)(2,1)} %all-to-all-done.5.out_parts.sums_ref.recv, f32[128,1024]{1,0:T(8,128)} %get-tuple-element.148.q_ref, f32[128,512]{1,0:T(8,128)} %get-tuple-element.149.k_ref, bf16[128,1024]{1,0:T(8,128)(2,1)} %bitcast.89, ...), custom_call_target="tpu_custom_call" | custom-call | flops 536870912 | bytes 8388608 | tf_op jit(solution)/shard_map/input_back/pallas_call | solution.py:680
  279.5 8.6 %all-to-all-start.7 = ((bf16[64,208,128]{2,1,0:T(8,128)(2,1)}), bf16[64,208,128]{2,1,0:T(8,128)(2,1)}, u32[]{:S(2)}, u32[]{:S(2)}) async-start(bf16[64,208,128]{2,1,0:T(8,128)(2,1)} %share_out.1), calls=%async_computation.7 | async-start | bytes 6815744 | tf_op jit(solution)/shard_map/all_to_all | solution.py:906
  298.8 30.6 %all-to-all-done.7 = bf16[64,208,128]{2,1,0:T(8,128)(2,1)} async-done(((bf16[64,208,128]{2,1,0:T(8,128)(2,1)}), bf16[64,208,128]{2,1,0:T(8,128)(2,1)}, u32[]{:S(2)}, u32[]{:S(2)}) %all-to-all-start.7) | async-done | bytes 3407904 | tf_op jit(solution)/shard_map/all_to_all | solution.py:906
  333.7 5.4 %spread.2 = (f32[4,2,128,1024]{3,2,1,0:T(8,128)}, f32[4,2,128,512]{3,2,1,0:T(8,128)}, f32[4,2,128,512]{3,2,1,0:T(8,128)}, f32[4,2,128,1024]{3,2,1,0:T(8,128)}, f...) custom-call(s32[1]{0:T(128)} %bitcast.2.place, ...), custom_call_target="tpu_custom_call" | custom-call | tf_op jit(solution)/shard_map/spread/pallas_call | solution.py:861
  339.7 5.6 %spread.3 = (f32[4,2,128,1024]{3,2,1,0:T(8,128)}, f32[4,2,128,512]{3,2,1,0:T(8,128)}, f32[4,2,128,512]{3,2,1,0:T(8,128)}, f32[4,2,128,1024]{3,2,1,0:T(8,128)}, f...) custom-call(s32[1]{0:T(128)} %bitcast.34.place, ...), custom_call_target="tpu_custom_call", output_to_operand_aliasing={{0}: (2, {}), {1}: (3, {}), {2}: (4, {}), {3}: (5, {})} | custom-call | tf_op jit(solution)/shard_map/spread/pallas_call | solution.py:861
  (109 shorter events, 90.9 us)
Async XLA Ops:
  7.2 41.8 %copy-start = (bf16[2,128,1024]{2,1,0:T(8,128)(2,1)S(1)}, bf16[2,128,1024]{2,1,0:T(8,128)(2,1)}, u32[]{:S(2)}) copy-start(bf16[2,128,1024]{2,1,0:T(8,128)(2,1)} %param.35) | copy-start | bytes 1572868
  7.2 90.7 %all-gather.4.cloned.1.call-start = ((), (), s32[]{:S(2)}) async-start(), calls=%async_computation.9 | async-start | bytes 4456448 | tf_op jit(solution)/shard_map/all_gather | solution.py:956
  12.2 23.5 %all-to-all-start = ((bf16[16,208,128]{2,1,0:T(8,128)(2,1)}), bf16[16,208,128]{2,1,0:T(8,128)(2,1)S(1)}, u32[]{:S(2)}, u32[]{:S(2)}) async-start(bf16[16,208,128]{2,1,0:T(8,128)(2,1)} %get-tuple-element.98), calls=%async_computation | async-start | bytes 1703936 | tf_op jit(solution)/shard_map/all_to_all | solution.py:882
  43.9 13.9 %all-to-all-start.1 = ((bf16[16,64,128]{2,1,0:T(8,128)(2,1)}), bf16[16,64,128]{2,1,0:T(8,128)(2,1)S(1)}, u32[]{:S(2)}, u32[]{:S(2)}) async-start(bf16[16,64,128]{2,1,0:T(8,128)(2,1)} %get-tuple-element.101), calls=%async_computation.1 | async-start | bytes 524288 | tf_op jit(solution)/shard_map/all_to_all | solution.py:882
  48.9 109.3 %all-gather.6.cloned.1.call-start = ((), (), s32[]{:S(2)}) async-start(), calls=%async_computation.10 | async-start | bytes 4456448 | tf_op jit(solution)/shard_map/all_gather | solution.py:967
  57.8 33.0 %collective-permute-start.1 = (bf16[2,3072,128]{2,1,0:T(8,128)(2,1)}, bf16[2,3072,128]{2,1,0:T(8,128)(2,1)}, u32[]{:S(2)}, u32[]{:S(2)}) collective-permute-start(bf16[2,3072,128]{2,1,0:T(8,128)(2,1)} %pad_maximum_fusion.refs_0_), channel_id=1, source_target_pairs={{0,66},{1,67},{2,64},{3,65},{64,2},{65,3},{66,0},{67,1},{4,70},{5,... | collective-permute-start | bytes 4718600 | tf_op jit(solution)/shard_map/ppermute | solution.py:892
  65.6 37.9 %all-to-all-start.2 = ((bf16[16,2,40,1024]{3,2,1,0:T(8,128)(2,1)}), bf16[16,2,40,1024]{3,2,1,0:T(8,128)(2,1)}, u32[]{:S(2)}, u32[]{:S(2)}) async-start(bf16[16,2,40,1024]{3,2,1,0:T(8,128)(2,1)} %bitcast.86), calls=%async_computation.2 | async-start | bytes 5242880 | tf_op jit(solution)/shard_map/all_to_all | solution.py:882
  70.4 33.1 %collective-permute-start = (bf16[2,3072,128]{2,1,0:T(8,128)(2,1)}, bf16[2,3072,128]{2,1,0:T(8,128)(2,1)}, u32[]{:S(2)}, u32[]{:S(2)}) collective-permute-start(bf16[2,3072,128]{2,1,0:T(8,128)(2,1)} %pad_maximum_fusion.refs_0_), channel_id=1, source_target_pairs={{0,1},{1,0},{2,3},{3,2},{4,5},{5,4},{6,7},{7,6},{8,9},{9,8},{10,11... | collective-permute-start | bytes 4718600 | tf_op jit(solution)/shard_map/ppermute | solution.py:887
  90.9 12.7 %collective-permute-start.2 = (bf16[2,3072,128]{2,1,0:T(8,128)(2,1)}, bf16[2,3072,128]{2,1,0:T(8,128)(2,1)}, u32[]{:S(2)}, u32[]{:S(2)}) collective-permute-start(bf16[2,3072,128]{2,1,0:T(8,128)(2,1)} %collective-permute-done.1.refs_2_), channel_id=1, source_target_pairs={{0,1},{1,0},{2,3},{3,2},{4,5},{5,4},{6,7},{7,6},{8,9},{9,8},{10,11... | collective-permute-start | bytes 4718600 | tf_op jit(solution)/shard_map/ppermute | solution.py:887
  97.6 5.9 %collective-permute-start.3 = (bf16[128,512]{1,0:T(8,128)(2,1)S(1)}, bf16[128,512]{1,0:T(8,128)(2,1)S(1)}, u32[]{:S(2)}, u32[]{:S(2)}) collective-permute-start(bf16[128,512]{1,0:T(8,128)(2,1)S(1)} %bitcast.98), channel_id=1, source_target_pairs={{0,1},{1,0},{2,3},{3,2},{4,5},{5,4},{6,7},{7,6},{8,9},{9,8},{10,11... | collective-permute-start | bytes 393224 | tf_op jit(solution)/shard_map/ppermute | solution.py:887
  117.5 50.8 %all-to-all-start.3 = ((bf16[16,2,40,1152]{3,2,1,0:T(8,128)(2,1)}), bf16[16,2,40,1152]{3,2,1,0:T(8,128)(2,1)}, u32[]{:S(2)}, u32[]{:S(2)}) async-start(bf16[16,2,40,1152]{3,2,1,0:T(8,128)(2,1)} %experts.1), calls=%async_computation.3 | async-start | bytes 5898240 | tf_op jit(solution)/shard_map/all_to_all | solution.py:882
  122.9 174.0 %reduce-scatter.4.cloned.1.call-start = ((), (), s32[]{:S(2)}) async-start(), calls=%async_computation.11 | async-start | bytes 4456448
  168.2 21.4 %collective-permute-start.4 = (bf16[2,2,3072,128]{3,2,1,0:T(8,128)(2,1)}, bf16[2,2,3072,128]{3,2,1,0:T(8,128)(2,1)}, u32[]{:S(2)}, u32[]{:S(2)}) collective-permute-start(bf16[2,2,3072,128]{3,2,1,0:T(8,128)(2,1)} %get-tuple-element.128), channel_id=1, source_target_pairs={{0,1},{1,0},{2,3},{3,2},{4,5},{5,4},{6,7},{7,6},{8,9},{9,8},{10,11... | collective-permute-start | bytes 9437192 | tf_op jit(solution)/shard_map/ppermute | solution.py:887
  181.6 4.4 %collective-permute-start.5 = (bf16[128,1024]{1,0:T(8,128)(2,1)S(1)}, bf16[128,1024]{1,0:T(8,128)(2,1)S(1)}, u32[]{:S(2)}, u32[]{:S(2)}) collective-permute-start(bf16[128,1024]{1,0:T(8,128)(2,1)S(1)} %convert_element_type.133), channel_id=1, source_target_pairs={{0,1},{1,0},{2,3},{3,2},{4,5},{5,4},{6,7},{7,6},{8,9},{9,8},{10,11... | collective-permute-start | bytes 786440 | tf_op jit(solution)/shard_map/ppermute | solution.py:887
  182.3 13.4 %all-to-all-start.4 = ((bf16[16,96,128]{2,1,0:T(8,128)(2,1)}), bf16[16,96,128]{2,1,0:T(8,128)(2,1)S(1)}, u32[]{:S(2)}, u32[]{:S(2)}) async-start(bf16[16,96,128]{2,1,0:T(8,128)(2,1)} %get-tuple-element.126), calls=%async_computation.4 | async-start | bytes 786432 | tf_op jit(solution)/shard_map/all_to_all | solution.py:882
  195.7 28.5 %collective-permute-start.6 = (bf16[3072,128]{1,0:T(8,128)(2,1)}, bf16[3072,128]{1,0:T(8,128)(2,1)}, u32[]{:S(2)}, u32[]{:S(2)}) collective-permute-start(bf16[3072,128]{1,0:T(8,128)(2,1)} %get-tuple-element.141), channel_id=1, source_target_pairs={{0,66},{1,67},{2,64},{3,65},{64,2},{65,3},{66,0},{67,1},{4,70},{5,... | collective-permute-start | bytes 2359304 | tf_op jit(solution)/shard_map/ppermute | solution.py:892
  198.8 32.4 %collective-permute-start.7 = (bf16[3072,128]{1,0:T(8,128)(2,1)}, bf16[3072,128]{1,0:T(8,128)(2,1)}, u32[]{:S(2)}, u32[]{:S(2)}) collective-permute-start(bf16[3072,128]{1,0:T(8,128)(2,1)} %get-tuple-element.143), channel_id=1, source_target_pairs={{0,66},{1,67},{2,64},{3,65},{64,2},{65,3},{66,0},{67,1},{4,70},{5,... | collective-permute-start | bytes 2359304 | tf_op jit(solution)/shard_map/ppermute | solution.py:892
  218.4 36.9 %all-to-all-start.5 = ((bf16[16,480,128]{2,1,0:T(8,128)(2,1)}), bf16[16,480,128]{2,1,0:T(8,128)(2,1)}, u32[]{:S(2)}, u32[]{:S(2)}) async-start(bf16[16,480,128]{2,1,0:T(8,128)(2,1)} %get-tuple-element.139.early.later.queries), calls=%async_computation.5 | async-start | bytes 3932160 | tf_op jit(solution)/shard_map/all_to_all | solution.py:882
  226.5 28.8 %collective-permute-start.9 = (bf16[3072,128]{1,0:T(8,128)(2,1)}, bf16[3072,128]{1,0:T(8,128)(2,1)}, u32[]{:S(2)}, u32[]{:S(2)}) collective-permute-start(bf16[3072,128]{1,0:T(8,128)(2,1)} %add_convert_fusion.1), channel_id=1, source_target_pairs={{0,64},{64,0},{1,65},{65,1},{2,66},{66,2},{3,67},{67,3},{4,68},{68... | collective-permute-start | bytes 2359304 | tf_op jit(solution)/shard_map/ppermute | solution.py:887
  233.4 29.4 %collective-permute-start.10 = (bf16[3072,128]{1,0:T(8,128)(2,1)}, bf16[3072,128]{1,0:T(8,128)(2,1)S(1)}, u32[]{:S(2)}, u32[]{:S(2)}) collective-permute-start(bf16[3072,128]{1,0:T(8,128)(2,1)} %add_convert_fusion), channel_id=1, source_target_pairs={{0,64},{64,0},{1,65},{65,1},{2,66},{66,2},{3,67},{67,3},{4,68},{68... | collective-permute-start | bytes 2359304 | tf_op jit(solution)/shard_map/ppermute | solution.py:887
  233.5 21.9 %collective-permute-start.8 = (bf16[16,64,128]{2,1,0:T(8,128)(2,1)S(1)}, bf16[16,64,128]{2,1,0:T(8,128)(2,1)S(1)}, u32[]{:S(2)}, u32[]{:S(2)}) collective-permute-start(bf16[16,64,128]{2,1,0:T(8,128)(2,1)S(1)} %copy-done.19), channel_id=1, source_target_pairs={{0,4},{4,0},{8,12},{12,8},{16,20},{20,16},{24,28},{28,24},{32,36},... | collective-permute-start | bytes 786440 | tf_op jit(solution)/shard_map/ppermute | solution.py:887
  262.8 13.0 %all-to-all-start.6 = ((bf16[8,208,128]{2,1,0:T(8,128)(2,1)}), bf16[8,208,128]{2,1,0:T(8,128)(2,1)S(1)}, u32[]{:S(2)}, u32[]{:S(2)}) async-start(bf16[8,208,128]{2,1,0:T(8,128)(2,1)} %head_grads.1), calls=%async_computation.6 | async-start | bytes 851968 | tf_op jit(solution)/shard_map/all_to_all | solution.py:1021
  279.5 49.9 %all-to-all-start.7 = ((bf16[64,208,128]{2,1,0:T(8,128)(2,1)}), bf16[64,208,128]{2,1,0:T(8,128)(2,1)}, u32[]{:S(2)}, u32[]{:S(2)}) async-start(bf16[64,208,128]{2,1,0:T(8,128)(2,1)} %share_out.1), calls=%async_computation.7 | async-start | bytes 6815744 | tf_op jit(solution)/shard_map/all_to_all | solution.py:906
  329.5 10.3 %collective-permute-start.11 = (bf16[64,208,128]{2,1,0:T(8,128)(2,1)}, bf16[64,208,128]{2,1,0:T(8,128)(2,1)}, u32[]{:S(2)}, u32[]{:S(2)}) collective-permute-start(bf16[64,208,128]{2,1,0:T(8,128)(2,1)} %all-to-all-done.7), channel_id=1, source_target_pairs={{0,1},{1,0},{2,3},{3,2},{4,5},{5,4},{6,7},{7,6},{8,9},{9,8},{10,11... | collective-permute-start | bytes 10223624 | tf_op jit(solution)/shard_map/ppermute | solution.py:887
  (19 other events, 142.3 us)
Sparse Core Ops, SparseCore 0:
  10.2 61.9 all-gather.3
  74.9 83.2 all-gather.5
  174.7 89.6 reduce-scatter.3
